TPU v7x, 128 devices: a whole 4x4x4 slice. The times are simulated.
128 devices in a mesh: ctx: 16 (over y, z), chan: 8 (over x, core).
Axes of the slice: x: 4, y: 4, z: 4, core: 2. Of those that a mesh axis runs over, the one named last changes fastest.
Arguments:
- tokens: bfloat16 [4096, 4096], P('ctx', 'chan'), may hold values from -6 to 6
- w_in: bfloat16 [4096, 3, 4096], P(None, None, 'chan'), may hold values from -0.09375 to 0.09375
- short_kernel: float32 [3, 3, 4096], P(None, None, 'chan'), may hold values from -3 to 3
- residue: float32 [4096, 16], P('chan'), may hold values from -2 to 2
- rate: float32 [4096, 16], P('chan'), as said below
- w_out: bfloat16 [4096, 4096], P(None, 'chan'), may hold values from -0.09375 to 0.09375
Outputs:
- mixed: bfloat16 [4096, 4096], P('ctx', 'chan')
Inputs may be any that keep to these rules, and one draw needn't show every extreme that they name: `rate`: all rates are positive.
All inputs are finite; a program needn't handle non-finite values.
Results may differ from a plain program's by a relative error of at most 0.0074.
Values may be sent and summed in bfloat16 or wider, within the bound.
A program may use at most 128 MiB of HBM per device.

v0:
```python
import jax
import jax.numpy as jnp
from jax import lax
from jax.sharding import PartitionSpec as P

SHORT = 3
LSUB = 64


exact = lax.Precision.HIGHEST


def shifted(value, axis, by):
    count = lax.axis_size(axis)
    pairs = [(i, i + by) for i in range(count) if 0 <= i + by < count]
    return lax.ppermute(value, axis, pairs)


def per_device(tokens, w_in, short_kernel, residue, rate, w_out):
    count = tokens.shape[0]
    model_width = w_in.shape[0]
    channels = w_in.shape[2]
    flat_in = w_in.reshape(model_width, 3 * channels)
    margin = SHORT - 1
    panel = flat_in
    summed = jnp.dot(
        lax.all_gather(tokens, "chan", axis=1, tiled=True),
        panel,
        preferred_element_type=jnp.float32,
    )
    own_rows = summed.astype(jnp.bfloat16)
    tail = shifted(own_rows[count - margin :], "ctx", 1)
    widened = jnp.concatenate([tail, own_rows], 0)
    widened = widened.reshape(count + margin, 3, channels)
    filtered = jnp.zeros((count, 3, channels), jnp.float32)
    for tap in range(SHORT):
        first = margin - tap
        filtered = filtered + short_kernel[tap] * widened[first : first + count].astype(jnp.float32)
    gated = (filtered[:, 1] * filtered[:, 2]).astype(jnp.bfloat16)
    sub = LSUB
    blocks_count = count // sub
    offsets = jnp.arange(sub, dtype=jnp.float32)
    power = jnp.exp(-rate[None] * offsets[:, None, None])
    weight = residue * jnp.sqrt(1.0 - jnp.exp(-2.0 * rate))
    impulse_rows = jnp.sum(jnp.transpose(power, (1, 0, 2)) * weight[:, None, :], axis=2)
    lagged = jnp.arange(sub)[:, None] - jnp.arange(sub)[None, :]
    toeplitz = jnp.where((lagged >= 0)[None], impulse_rows[:, jnp.clip(lagged, 0, sub - 1)], 0.0)
    tail_power = jnp.transpose(power[::-1], (1, 0, 2))
    readout = jnp.transpose(power * jnp.exp(-rate)[None] * weight[None], (1, 0, 2))
    index = jnp.arange(blocks_count, dtype=jnp.float32)
    final_weights = jnp.exp(-rate[None] * (sub * (blocks_count - 1 - index))[:, None, None])

    def sub_states(block):
        pieces = block.astype(jnp.float32).T.reshape(channels, blocks_count, sub)
        return (
            pieces,
            jnp.transpose(
                jnp.einsum("ckj,cjr->ckr", pieces, tail_power, precision=exact), (1, 0, 2)
            ),
        )

    def end_state(states):
        return jnp.sum(final_weights * states, axis=0)

    pieces, states = sub_states(gated)
    block_decay = jnp.exp(-rate * count)
    hops = lax.axis_size("ctx") - 1

    def relay(turn, carry):
        incoming, entry_state, factor = carry
        incoming = shifted(incoming, "ctx", 1)
        entry_state = entry_state + factor * end_state(sub_states(incoming)[1])
        return (incoming, entry_state, factor * block_decay)

    start_carry = (gated, jnp.zeros_like(rate), jnp.ones_like(rate))
    entry = lax.fori_loop(0, hops, relay, start_carry)[1]
    gaps = sub * (index[:, None] - 1.0 - index[None, :])
    earlier_mask = index[:, None] > index[None, :]
    carry_table = jnp.where(
        earlier_mask[:, :, None, None],
        jnp.exp(-rate[None, None] * jnp.maximum(gaps, 0.0)[:, :, None, None]),
        0.0,
    )
    entry_decay = jnp.exp(-rate[None] * (sub * index)[:, None, None])
    before_states = jnp.sum(carry_table * states[None], axis=1) + entry_decay * entry[None]
    within = jnp.einsum("ckj,cij->cki", pieces, toeplitz, precision=exact)
    across = jnp.einsum("kcr,cir->cki", before_states, readout, precision=exact)
    long_conv = (within + across).reshape(channels, count).T
    modulated = (filtered[:, 0] * long_conv).astype(jnp.bfloat16)
    panel = w_out
    mixed = jnp.dot(
        lax.all_gather(modulated, "chan", axis=1, tiled=True),
        panel,
        preferred_element_type=jnp.float32,
    )
    return mixed.astype(jnp.bfloat16)


def solution(mesh):
    in_specs = (
        P("ctx", "chan"),
        P(None, None, "chan"),
        P(None, None, "chan"),
        P("chan", None),
        P("chan", None),
        P(None, "chan"),
    )
    out_specs = P("ctx", "chan")
    return jax.shard_map(
        per_device, mesh=mesh, in_specs=in_specs, out_specs=out_specs, check_vma=False
    )
```

profile of v0, /device:TPU:25, one launch (start us, length us, event | category | flops | bytes accessed | tf_op | source)
XLA Modules:
  0.0 448.0 jit_solution(1915548090725706962)
XLA Ops:
  7.3 16.9 %copy.47 = bf16[4096,3,512]{0,2,1:T(8,128)(2,1)} copy(bf16[4096,3,512]{2,0,1:T(8,128)(2,1)} %param.9) | data formatting | bytes 25165824 | tf_op args[1]
  26.2 6.0 %multiply_reduce_fusion = f32[512,64]{1,0:T(8,128)S(1)} fusion(f32[512,16]{1,0:T(8,128)S(1)} %copy.53, f32[512,16]{1,0:T(8,128)S(1)} %get-tuple-element.192), kind=kLoop, calls=%fused_computation.16 | loop fusion | flops 1540096 | bytes 196608 | tf_op jit(solution)/shard_map/reduce_sum | solution.py:45
  36.7 8.7 %convolution_convert_fusion = bf16[256,1536]{1,0:T(8,128)(2,1)S(1)} fusion(bf16[256,4096]{1,0:T(8,128)(2,1)} %all-gather.3.cloned.1.call-done, bf16[4096,1536]{0,1:T(8,128)(2,1)} %bitcast.65), kind=kOutput, calls=%fused_computation.18 | convolution fusion | flops 3221618688 | bytes 15466496 | tf_op jit(solution)/shard_map/dot_general | solution.py:26
  50.2 16.8 %gather_fusion = f32[4096,512]{1,0:T(8,128)} fusion(f32[512,64]{0,1:T(8,128)S(1)} %copy.54, s32[4096]{0:T(1024)S(1)} %broadcast_clamp_fusion), kind=kCustom, calls=%fused_computation | custom fusion | bytes 16793600 | tf_op jit(solution)/shard_map/gather | solution.py:47
  66.9 16.2 %copy.55 = f32[64,64,512]{1,0,2:T(8,128)} copy(f32[64,64,512]{2,1,0:T(8,128)} %bitcast.63) | data formatting | bytes 16777216 | tf_op jit(solution)/shard_map/gather | solution.py:47
  83.2 7.2 %rev.3 = f32[64,512,16]{0,2,1:T(8,128)} reverse(f32[64,512,16]{0,2,1:T(8,128)} %multiply_exponential_fusion), dimensions={0} | reverse | bytes 4194304 | tf_op jit(solution)/shard_map/rev | solution.py:48
  104.6 6.7 %convolution_bitcast_fusion.1 = f32[4,512,16]{2,0,1:T(4,128)} fusion(bf16[512,4,64]{2,1,0:T(4,128)(2,1)S(1)} %copy.56, f32[64,512,16]{0,2,1:T(8,128)} %rev.3), kind=kOutput, calls=%fused_computation.24 | convolution fusion | flops 25165824 | bytes 2490368 | tf_op jit(solution)/shard_map/ckj,cjr->ckr/dot_general | solution.py:58
  113.7 251.1 %while.15 = (s32[]{:T(128)}, bf16[256,512]{1,0:T(8,128)(2,1)}, f32[512,16]{1,0:T(8,128)S(1)}, f32[512,16]{1,0:T(8,128)S(1)}, f32[512,64,16]{1,2,0:T(8,128)}, /*i...) while((s32[]{:T(128)}, bf16[256,512]{1,0:T(8,128)(2,1)}, ...), condition=%wide.region_4.5_spmd.clone, body=%wide.region_2.0_spmd.clone.sunk | while | flops 25296900 | bytes 4718767 | solution.py:76
  116.9 8.4 %collective-permute-done = bf16[256,512]{1,0:T(8,128)(2,1)S(1)} collective-permute-done((bf16[256,512]{1,0:T(8,128)(2,1)}, bf16[256,512]{1,0:T(8,128)(2,1)S(1)}, u32[]{:S(2)}, u32[]{:S(2)}) %collective-permute-start) | collective-permute-done | bytes 262176 | tf_op jit(solution)/shard_map/while/body/eval_jaxpr/ppermute | solution.py:16
  125.6 5.7 %fusion.42 = f32[512,16]{1,0:T(8,128)S(1)} fusion(bf16[512,4,64]{2,1,0:T(4,128)(2,1)S(1)} %copy.67, f32[512,64,16]{1,2,0:T(8,128)} %get-tuple-element.209, f32[4]{0:T(128)S(1)} %get-tuple-element.211, f32[512,16]{1,0:T(8,128)S(1)} %get-tuple-element.212), kind=kOutput, calls=%fused_computation.4.clone.1 | convolution fusion | flops 25255936 | bytes 2424848 | tf_op jit(solution)/shard_map/while/body/eval_jaxpr/ckj,cjr->ckr/dot_general | solution.py:58
  134.1 8.7 %collective-permute-done = bf16[256,512]{1,0:T(8,128)(2,1)S(1)} collective-permute-done((bf16[256,512]{1,0:T(8,128)(2,1)}, bf16[256,512]{1,0:T(8,128)(2,1)S(1)}, u32[]{:S(2)}, u32[]{:S(2)}) %collective-permute-start) | collective-permute-done | bytes 262176 | tf_op jit(solution)/shard_map/while/body/eval_jaxpr/ppermute | solution.py:16
  143.1 5.7 %fusion.42 = f32[512,16]{1,0:T(8,128)S(1)} fusion(bf16[512,4,64]{2,1,0:T(4,128)(2,1)S(1)} %copy.67, f32[512,64,16]{1,2,0:T(8,128)} %get-tuple-element.209, f32[4]{0:T(128)S(1)} %get-tuple-element.211, f32[512,16]{1,0:T(8,128)S(1)} %get-tuple-element.212), kind=kOutput, calls=%fused_computation.4.clone.1 | convolution fusion | flops 25255936 | bytes 2424848 | tf_op jit(solution)/shard_map/while/body/eval_jaxpr/ckj,cjr->ckr/dot_general | solution.py:58
  151.6 7.5 %collective-permute-done = bf16[256,512]{1,0:T(8,128)(2,1)S(1)} collective-permute-done((bf16[256,512]{1,0:T(8,128)(2,1)}, bf16[256,512]{1,0:T(8,128)(2,1)S(1)}, u32[]{:S(2)}, u32[]{:S(2)}) %collective-permute-start) | collective-permute-done | bytes 262176 | tf_op jit(solution)/shard_map/while/body/eval_jaxpr/ppermute | solution.py:16
  168.0 7.5 %collective-permute-done = bf16[256,512]{1,0:T(8,128)(2,1)S(1)} collective-permute-done((bf16[256,512]{1,0:T(8,128)(2,1)}, bf16[256,512]{1,0:T(8,128)(2,1)S(1)}, u32[]{:S(2)}, u32[]{:S(2)}) %collective-permute-start) | collective-permute-done | bytes 262176 | tf_op jit(solution)/shard_map/while/body/eval_jaxpr/ppermute | solution.py:16
  184.3 7.5 %collective-permute-done = bf16[256,512]{1,0:T(8,128)(2,1)S(1)} collective-permute-done((bf16[256,512]{1,0:T(8,128)(2,1)}, bf16[256,512]{1,0:T(8,128)(2,1)S(1)}, u32[]{:S(2)}, u32[]{:S(2)}) %collective-permute-start) | collective-permute-done | bytes 262176 | tf_op jit(solution)/shard_map/while/body/eval_jaxpr/ppermute | solution.py:16
  200.7 7.5 %collective-permute-done = bf16[256,512]{1,0:T(8,128)(2,1)S(1)} collective-permute-done((bf16[256,512]{1,0:T(8,128)(2,1)}, bf16[256,512]{1,0:T(8,128)(2,1)S(1)}, u32[]{:S(2)}, u32[]{:S(2)}) %collective-permute-start) | collective-permute-done | bytes 262176 | tf_op jit(solution)/shard_map/while/body/eval_jaxpr/ppermute | solution.py:16
  217.0 7.5 %collective-permute-done = bf16[256,512]{1,0:T(8,128)(2,1)S(1)} collective-permute-done((bf16[256,512]{1,0:T(8,128)(2,1)}, bf16[256,512]{1,0:T(8,128)(2,1)S(1)}, u32[]{:S(2)}, u32[]{:S(2)}) %collective-permute-start) | collective-permute-done | bytes 262176 | tf_op jit(solution)/shard_map/while/body/eval_jaxpr/ppermute | solution.py:16
  233.3 7.5 %collective-permute-done = bf16[256,512]{1,0:T(8,128)(2,1)S(1)} collective-permute-done((bf16[256,512]{1,0:T(8,128)(2,1)}, bf16[256,512]{1,0:T(8,128)(2,1)S(1)}, u32[]{:S(2)}, u32[]{:S(2)}) %collective-permute-start) | collective-permute-done | bytes 262176 | tf_op jit(solution)/shard_map/while/body/eval_jaxpr/ppermute | solution.py:16
  249.7 7.5 %collective-permute-done = bf16[256,512]{1,0:T(8,128)(2,1)S(1)} collective-permute-done((bf16[256,512]{1,0:T(8,128)(2,1)}, bf16[256,512]{1,0:T(8,128)(2,1)S(1)}, u32[]{:S(2)}, u32[]{:S(2)}) %collective-permute-start) | collective-permute-done | bytes 262176 | tf_op jit(solution)/shard_map/while/body/eval_jaxpr/ppermute | solution.py:16
  257.5 5.7 %fusion.42 = f32[512,16]{1,0:T(8,128)S(1)} fusion(bf16[512,4,64]{2,1,0:T(4,128)(2,1)S(1)} %copy.67, f32[512,64,16]{1,2,0:T(8,128)} %get-tuple-element.209, f32[4]{0:T(128)S(1)} %get-tuple-element.211, f32[512,16]{1,0:T(8,128)S(1)} %get-tuple-element.212), kind=kOutput, calls=%fused_computation.4.clone.1 | convolution fusion | flops 25255936 | bytes 2424848 | tf_op jit(solution)/shard_map/while/body/eval_jaxpr/ckj,cjr->ckr/dot_general | solution.py:58
  266.0 7.5 %collective-permute-done = bf16[256,512]{1,0:T(8,128)(2,1)S(1)} collective-permute-done((bf16[256,512]{1,0:T(8,128)(2,1)}, bf16[256,512]{1,0:T(8,128)(2,1)S(1)}, u32[]{:S(2)}, u32[]{:S(2)}) %collective-permute-start) | collective-permute-done | bytes 262176 | tf_op jit(solution)/shard_map/while/body/eval_jaxpr/ppermute | solution.py:16
  282.4 7.5 %collective-permute-done = bf16[256,512]{1,0:T(8,128)(2,1)S(1)} collective-permute-done((bf16[256,512]{1,0:T(8,128)(2,1)}, bf16[256,512]{1,0:T(8,128)(2,1)S(1)}, u32[]{:S(2)}, u32[]{:S(2)}) %collective-permute-start) | collective-permute-done | bytes 262176 | tf_op jit(solution)/shard_map/while/body/eval_jaxpr/ppermute | solution.py:16
  298.7 7.5 %collective-permute-done = bf16[256,512]{1,0:T(8,128)(2,1)S(1)} collective-permute-done((bf16[256,512]{1,0:T(8,128)(2,1)}, bf16[256,512]{1,0:T(8,128)(2,1)S(1)}, u32[]{:S(2)}, u32[]{:S(2)}) %collective-permute-start) | collective-permute-done | bytes 262176 | tf_op jit(solution)/shard_map/while/body/eval_jaxpr/ppermute | solution.py:16
  315.1 7.5 %collective-permute-done = bf16[256,512]{1,0:T(8,128)(2,1)S(1)} collective-permute-done((bf16[256,512]{1,0:T(8,128)(2,1)}, bf16[256,512]{1,0:T(8,128)(2,1)S(1)}, u32[]{:S(2)}, u32[]{:S(2)}) %collective-permute-start) | collective-permute-done | bytes 262176 | tf_op jit(solution)/shard_map/while/body/eval_jaxpr/ppermute | solution.py:16
  322.9 5.7 %fusion.42 = f32[512,16]{1,0:T(8,128)S(1)} fusion(bf16[512,4,64]{2,1,0:T(4,128)(2,1)S(1)} %copy.67, f32[512,64,16]{1,2,0:T(8,128)} %get-tuple-element.209, f32[4]{0:T(128)S(1)} %get-tuple-element.211, f32[512,16]{1,0:T(8,128)S(1)} %get-tuple-element.212), kind=kOutput, calls=%fused_computation.4.clone.1 | convolution fusion | flops 25255936 | bytes 2424848 | tf_op jit(solution)/shard_map/while/body/eval_jaxpr/ckj,cjr->ckr/dot_general | solution.py:58
  331.4 8.3 %collective-permute-done = bf16[256,512]{1,0:T(8,128)(2,1)S(1)} collective-permute-done((bf16[256,512]{1,0:T(8,128)(2,1)}, bf16[256,512]{1,0:T(8,128)(2,1)S(1)}, u32[]{:S(2)}, u32[]{:S(2)}) %collective-permute-start) | collective-permute-done | bytes 262176 | tf_op jit(solution)/shard_map/while/body/eval_jaxpr/ppermute | solution.py:16
  340.0 5.7 %fusion.42 = f32[512,16]{1,0:T(8,128)S(1)} fusion(bf16[512,4,64]{2,1,0:T(4,128)(2,1)S(1)} %copy.67, f32[512,64,16]{1,2,0:T(8,128)} %get-tuple-element.209, f32[4]{0:T(128)S(1)} %get-tuple-element.211, f32[512,16]{1,0:T(8,128)S(1)} %get-tuple-element.212), kind=kOutput, calls=%fused_computation.4.clone.1 | convolution fusion | flops 25255936 | bytes 2424848 | tf_op jit(solution)/shard_map/while/body/eval_jaxpr/ckj,cjr->ckr/dot_general | solution.py:58
  348.5 9.4 %collective-permute-done = bf16[256,512]{1,0:T(8,128)(2,1)S(1)} collective-permute-done((bf16[256,512]{1,0:T(8,128)(2,1)}, bf16[256,512]{1,0:T(8,128)(2,1)S(1)}, u32[]{:S(2)}, u32[]{:S(2)}) %collective-permute-start) | collective-permute-done | bytes 262176 | tf_op jit(solution)/shard_map/while/body/eval_jaxpr/ppermute | solution.py:16
  358.2 5.7 %fusion.42 = f32[512,16]{1,0:T(8,128)S(1)} fusion(bf16[512,4,64]{2,1,0:T(4,128)(2,1)S(1)} %copy.67, f32[512,64,16]{1,2,0:T(8,128)} %get-tuple-element.209, f32[4]{0:T(128)S(1)} %get-tuple-element.211, f32[512,16]{1,0:T(8,128)S(1)} %get-tuple-element.212), kind=kOutput, calls=%fused_computation.4.clone.1 | convolution fusion | flops 25255936 | bytes 2424848 | tf_op jit(solution)/shard_map/while/body/eval_jaxpr/ckj,cjr->ckr/dot_general | solution.py:58
  368.0 17.0 %fusion.4 = f32[512,4,64]{2,1,0:T(4,128)S(1)} fusion(bf16[512,4,64]{2,1,0:T(4,128)(2,1)} %copy-done, f32[64,64,512]{1,0,2:T(8,128)} %copy.55, pred[64,64]{1,0:T(8,128)(4,1)S(1)} %subtract_compare_fusion), kind=kOutput, calls=%fused_computation.7 | convolution fusion | flops 102760448 | bytes 9179136 | tf_op jit(solution)/shard_map/ckj,cij->cki/dot_general | solution.py:86
  385.1 8.2 %fusion.15 = f32[512,4,64]{2,1,0:T(4,128)} fusion(f32[512,4,64]{2,1,0:T(4,128)S(1)} %fusion.4, f32[4,512,16]{2,0,1:T(4,128)S(1)} %copy-done.2, f32[512,16]{1,0:T(8,128)S(1)} %copy-done.5, f32[512,16]{1,0:T(8,128)S(1)} %copy-done.4, f32[512,16]{1,0:T(8,128)S(1)} %get-tuple-element.218), kind=kOutput, calls=%fused_computation.23 | convolution fusion | flops 26869760 | bytes 1277952 | tf_op jit(solution)/shard_map/kcr,cir->cki/dot_general | solution.py:87
  395.8 40.6 %all-gather.5.cloned.1.call-done = bf16[256,4096]{0,1:T(8,128)(2,1)} async-done(((bf16[256,512]{0,1:T(8,128)(2,1)}), bf16[256,4096]{0,1:T(8,128)(2,1)}) %all-gather.5.cloned.1.call-update) | async-done | bytes 2097168 | tf_op jit(solution)/shard_map/all_gather | solution.py:92
  (133 shorter events, 138.2 us)
Async XLA Ops:
  6.5 30.2 %all-gather.3.cloned.1.call-start = ((), (), s32[]{:S(2)}) async-start(), calls=%async_computation | async-start | bytes 2359296 | tf_op jit(solution)/shard_map/all_gather | solution.py:27
  7.3 17.0 %copy-start.6 = (f32[512,16]{0,1:T(8,128)S(1)}, f32[512,16]{0,1:T(8,128)}, u32[]{:S(2)}) copy-start(f32[512,16]{0,1:T(8,128)} %param.12) | copy-start | bytes 98308
  7.3 17.1 %copy-start.7 = (f32[512,16]{0,1:T(8,128)S(1)}, f32[512,16]{0,1:T(8,128)}, u32[]{:S(2)}) copy-start(f32[512,16]{0,1:T(8,128)} %param.11) | copy-start | bytes 98308
  7.3 18.1 %copy-start.8 = (f32[3,3,512]{2,1,0:T(4,128)S(1)}, f32[3,3,512]{2,1,0:T(4,128)}, u32[]{:S(2)}) copy-start(f32[3,3,512]{2,1,0:T(4,128)} %param.10) | copy-start | bytes 55300
  7.3 429.1 %all-gather.5.cloned.1.call-start = ((), (), s32[]{:S(2)}) async-start(), calls=%async_computation.1 | async-start | bytes 2359296 | tf_op jit(solution)/shard_map/all_gather | solution.py:92
  24.6 20.8 %copy-start.3 = (f32[512,16]{1,0:T(8,128)}, f32[512,16]{1,0:T(8,128)S(1)}, u32[]{:S(2)}) copy-start(f32[512,16]{1,0:T(8,128)S(1)} %copy.53) | copy-start | bytes 98308
  45.4 45.0 %copy-start.1 = (bf16[256,1536]{1,0:T(8,128)(2,1)}, bf16[256,1536]{1,0:T(8,128)(2,1)S(1)}, u32[]{:S(2)}) copy-start(bf16[256,1536]{1,0:T(8,128)(2,1)S(1)} %convolution_convert_fusion) | copy-start | bytes 2359300
  45.4 46.4 %collective-permute-start.1 = (bf16[2,1536]{1,0:T(2,128)(2,1)S(1)}, bf16[2,1536]{1,0:T(2,128)(2,1)S(1)}, u32[]{:S(2)}, u32[]{:S(2)}) collective-permute-start(bf16[2,1536]{1,0:T(2,128)(2,1)S(1)} %slice.42), channel_id=1, source_target_pairs={{0,8},{8,16},{16,24},{24,32},{32,40},{40,48},{48,56},{56,64},{64,7... | collective-permute-start | bytes 18440 | tf_op jit(solution)/shard_map/ppermute | solution.py:16
  104.6 9.1 %copy-start = (bf16[512,4,64]{2,1,0:T(4,128)(2,1)}, bf16[512,4,64]{2,1,0:T(4,128)(2,1)S(1)}, u32[]{:S(2)}) copy-start(bf16[512,4,64]{2,1,0:T(4,128)(2,1)S(1)} %copy.56) | copy-start | bytes 786436
  113.7 11.5 %collective-permute-start = (bf16[256,512]{1,0:T(8,128)(2,1)}, bf16[256,512]{1,0:T(8,128)(2,1)S(1)}, u32[]{:S(2)}, u32[]{:S(2)}) collective-permute-start(bf16[256,512]{1,0:T(8,128)(2,1)} %get-tuple-element.196), channel_id=1, source_target_pairs={{0,8},{8,16},{16,24},{24,32},{32,40},{40,48},{48,56},{56,64},{64,7... | collective-permute-start | bytes 786440 | tf_op jit(solution)/shard_map/while/body/eval_jaxpr/ppermute | solution.py:16
  132.2 10.6 %collective-permute-start = (bf16[256,512]{1,0:T(8,128)(2,1)}, bf16[256,512]{1,0:T(8,128)(2,1)S(1)}, u32[]{:S(2)}, u32[]{:S(2)}) collective-permute-start(bf16[256,512]{1,0:T(8,128)(2,1)} %get-tuple-element.196), channel_id=1, source_target_pairs={{0,8},{8,16},{16,24},{24,32},{32,40},{40,48},{48,56},{56,64},{64,7... | collective-permute-start | bytes 786440 | tf_op jit(solution)/shard_map/while/body/eval_jaxpr/ppermute | solution.py:16
  149.7 9.4 %collective-permute-start = (bf16[256,512]{1,0:T(8,128)(2,1)}, bf16[256,512]{1,0:T(8,128)(2,1)S(1)}, u32[]{:S(2)}, u32[]{:S(2)}) collective-permute-start(bf16[256,512]{1,0:T(8,128)(2,1)} %get-tuple-element.196), channel_id=1, source_target_pairs={{0,8},{8,16},{16,24},{24,32},{32,40},{40,48},{48,56},{56,64},{64,7... | collective-permute-start | bytes 786440 | tf_op jit(solution)/shard_map/while/body/eval_jaxpr/ppermute | solution.py:16
  166.1 9.4 %collective-permute-start = (bf16[256,512]{1,0:T(8,128)(2,1)}, bf16[256,512]{1,0:T(8,128)(2,1)S(1)}, u32[]{:S(2)}, u32[]{:S(2)}) collective-permute-start(bf16[256,512]{1,0:T(8,128)(2,1)} %get-tuple-element.196), channel_id=1, source_target_pairs={{0,8},{8,16},{16,24},{24,32},{32,40},{40,48},{48,56},{56,64},{64,7... | collective-permute-start | bytes 786440 | tf_op jit(solution)/shard_map/while/body/eval_jaxpr/ppermute | solution.py:16
  182.4 9.4 %collective-permute-start = (bf16[256,512]{1,0:T(8,128)(2,1)}, bf16[256,512]{1,0:T(8,128)(2,1)S(1)}, u32[]{:S(2)}, u32[]{:S(2)}) collective-permute-start(bf16[256,512]{1,0:T(8,128)(2,1)} %get-tuple-element.196), channel_id=1, source_target_pairs={{0,8},{8,16},{16,24},{24,32},{32,40},{40,48},{48,56},{56,64},{64,7... | collective-permute-start | bytes 786440 | tf_op jit(solution)/shard_map/while/body/eval_jaxpr/ppermute | solution.py:16
  198.7 9.4 %collective-permute-start = (bf16[256,512]{1,0:T(8,128)(2,1)}, bf16[256,512]{1,0:T(8,128)(2,1)S(1)}, u32[]{:S(2)}, u32[]{:S(2)}) collective-permute-start(bf16[256,512]{1,0:T(8,128)(2,1)} %get-tuple-element.196), channel_id=1, source_target_pairs={{0,8},{8,16},{16,24},{24,32},{32,40},{40,48},{48,56},{56,64},{64,7... | collective-permute-start | bytes 786440 | tf_op jit(solution)/shard_map/while/body/eval_jaxpr/ppermute | solution.py:16
  215.1 9.4 %collective-permute-start = (bf16[256,512]{1,0:T(8,128)(2,1)}, bf16[256,512]{1,0:T(8,128)(2,1)S(1)}, u32[]{:S(2)}, u32[]{:S(2)}) collective-permute-start(bf16[256,512]{1,0:T(8,128)(2,1)} %get-tuple-element.196), channel_id=1, source_target_pairs={{0,8},{8,16},{16,24},{24,32},{32,40},{40,48},{48,56},{56,64},{64,7... | collective-permute-start | bytes 786440 | tf_op jit(solution)/shard_map/while/body/eval_jaxpr/ppermute | solution.py:16
  231.4 9.4 %collective-permute-start = (bf16[256,512]{1,0:T(8,128)(2,1)}, bf16[256,512]{1,0:T(8,128)(2,1)S(1)}, u32[]{:S(2)}, u32[]{:S(2)}) collective-permute-start(bf16[256,512]{1,0:T(8,128)(2,1)} %get-tuple-element.196), channel_id=1, source_target_pairs={{0,8},{8,16},{16,24},{24,32},{32,40},{40,48},{48,56},{56,64},{64,7... | collective-permute-start | bytes 786440 | tf_op jit(solution)/shard_map/while/body/eval_jaxpr/ppermute | solution.py:16
  247.8 9.4 %collective-permute-start = (bf16[256,512]{1,0:T(8,128)(2,1)}, bf16[256,512]{1,0:T(8,128)(2,1)S(1)}, u32[]{:S(2)}, u32[]{:S(2)}) collective-permute-start(bf16[256,512]{1,0:T(8,128)(2,1)} %get-tuple-element.196), channel_id=1, source_target_pairs={{0,8},{8,16},{16,24},{24,32},{32,40},{40,48},{48,56},{56,64},{64,7... | collective-permute-start | bytes 786440 | tf_op jit(solution)/shard_map/while/body/eval_jaxpr/ppermute | solution.py:16
  264.1 9.4 %collective-permute-start = (bf16[256,512]{1,0:T(8,128)(2,1)}, bf16[256,512]{1,0:T(8,128)(2,1)S(1)}, u32[]{:S(2)}, u32[]{:S(2)}) collective-permute-start(bf16[256,512]{1,0:T(8,128)(2,1)} %get-tuple-element.196), channel_id=1, source_target_pairs={{0,8},{8,16},{16,24},{24,32},{32,40},{40,48},{48,56},{56,64},{64,7... | collective-permute-start | bytes 786440 | tf_op jit(solution)/shard_map/while/body/eval_jaxpr/ppermute | solution.py:16
  280.5 9.4 %collective-permute-start = (bf16[256,512]{1,0:T(8,128)(2,1)}, bf16[256,512]{1,0:T(8,128)(2,1)S(1)}, u32[]{:S(2)}, u32[]{:S(2)}) collective-permute-start(bf16[256,512]{1,0:T(8,128)(2,1)} %get-tuple-element.196), channel_id=1, source_target_pairs={{0,8},{8,16},{16,24},{24,32},{32,40},{40,48},{48,56},{56,64},{64,7... | collective-permute-start | bytes 786440 | tf_op jit(solution)/shard_map/while/body/eval_jaxpr/ppermute | solution.py:16
  296.8 9.4 %collective-permute-start = (bf16[256,512]{1,0:T(8,128)(2,1)}, bf16[256,512]{1,0:T(8,128)(2,1)S(1)}, u32[]{:S(2)}, u32[]{:S(2)}) collective-permute-start(bf16[256,512]{1,0:T(8,128)(2,1)} %get-tuple-element.196), channel_id=1, source_target_pairs={{0,8},{8,16},{16,24},{24,32},{32,40},{40,48},{48,56},{56,64},{64,7... | collective-permute-start | bytes 786440 | tf_op jit(solution)/shard_map/while/body/eval_jaxpr/ppermute | solution.py:16
  313.1 9.4 %collective-permute-start = (bf16[256,512]{1,0:T(8,128)(2,1)}, bf16[256,512]{1,0:T(8,128)(2,1)S(1)}, u32[]{:S(2)}, u32[]{:S(2)}) collective-permute-start(bf16[256,512]{1,0:T(8,128)(2,1)} %get-tuple-element.196), channel_id=1, source_target_pairs={{0,8},{8,16},{16,24},{24,32},{32,40},{40,48},{48,56},{56,64},{64,7... | collective-permute-start | bytes 786440 | tf_op jit(solution)/shard_map/while/body/eval_jaxpr/ppermute | solution.py:16
  329.5 10.2 %collective-permute-start = (bf16[256,512]{1,0:T(8,128)(2,1)}, bf16[256,512]{1,0:T(8,128)(2,1)S(1)}, u32[]{:S(2)}, u32[]{:S(2)}) collective-permute-start(bf16[256,512]{1,0:T(8,128)(2,1)} %get-tuple-element.196), channel_id=1, source_target_pairs={{0,8},{8,16},{16,24},{24,32},{32,40},{40,48},{48,56},{56,64},{64,7... | collective-permute-start | bytes 786440 | tf_op jit(solution)/shard_map/while/body/eval_jaxpr/ppermute | solution.py:16
  346.6 11.3 %collective-permute-start = (bf16[256,512]{1,0:T(8,128)(2,1)}, bf16[256,512]{1,0:T(8,128)(2,1)S(1)}, u32[]{:S(2)}, u32[]{:S(2)}) collective-permute-start(bf16[256,512]{1,0:T(8,128)(2,1)} %get-tuple-element.196), channel_id=1, source_target_pairs={{0,8},{8,16},{16,24},{24,32},{32,40},{40,48},{48,56},{56,64},{64,7... | collective-permute-start | bytes 786440 | tf_op jit(solution)/shard_map/while/body/eval_jaxpr/ppermute | solution.py:16
  368.0 17.0 %copy-start.2 = (f32[4,512,16]{2,0,1:T(4,128)S(1)}, f32[4,512,16]{2,0,1:T(4,128)}, u32[]{:S(2)}) copy-start(f32[4,512,16]{2,0,1:T(4,128)} %copy.63) | copy-start | bytes 393220
  368.0 17.0 %copy-start.4 = (f32[512,16]{1,0:T(8,128)S(1)}, f32[512,16]{1,0:T(8,128)}, u32[]{:S(2)}) copy-start(f32[512,16]{1,0:T(8,128)} %copy-done.3) | copy-start | bytes 98308
  368.0 17.0 %copy-start.5 = (f32[512,16]{1,0:T(8,128)S(1)}, f32[512,16]{1,0:T(8,128)}, u32[]{:S(2)}) copy-start(f32[512,16]{1,0:T(8,128)} %get-tuple-element.126) | copy-start | bytes 98308
Sparse Core Ops, SparseCore 0:
  9.0 27.6 all-gather.2
  396.0 40.3 all-gather.4
where the time goes:
time: 451 us; the launch traced here: 448 us
  waiting for transfers between devices  159 us (35%)
  matrix products  131 us (29%)
  local copies, waits for them, and re-layouts  87.4 us (19%)
  starting transfers between devices  33.3 us (7%)
  other arithmetic  22.7 us (5%)
  between operations  13.6 us (3%)
    ppermute x16, waiting for transfers between devices, shifted(): return lax.ppermute(value, axis, pairs)  117 us
    dot_general x16, matrix products, sub_states(): jnp.einsum('ckj,cjr->ckr', pieces, tail_power, precision=exact)  92.4 us
    all_gather x1, waiting for transfers between devices, per_device(): lax.all_gather(modulated, 'chan', axis=1, tiled=True)  40.6 us
    ppermute x16, starting transfers between devices, shifted(): return lax.ppermute(value, axis, pairs)  33.2 us
    gather x2, local copies, waits for them, and re-layouts, per_device(): impulse_rows[:, jnp.clip(lagged, 0, sub - 1)]  33 us
    unnamed x21, local copies, waits for them, and re-layouts  18 us
    dot_general x1, matrix products, per_device(): within = jnp.einsum('ckj,cij->cki', pieces, toeplitz, precision=exact)  17 us
    while x15, local copies, waits for them, and re-layouts  10.6 us
  transfers between devices with their start and end apart: 18, of which 17 were waited for; matrix products, arithmetic and copies ran while one was open for 16% of the time, Pallas kernels for 0%

commit v1 on v0

v1 whole, which is shorter than its diff:
```python
import functools

import jax
import jax.numpy as jnp
from jax import lax
from jax.experimental import pallas as pl
from jax.experimental.pallas import tpu as pltpu
from jax.sharding import PartitionSpec as P

MESH = pl.DeviceIdType.MESH
F32 = jnp.float32
BF16 = jnp.bfloat16
CTX = 16
ROWS = 256
WIDE = 512
BLOCKS = 8
MODES = 16
SHORT = 3
SUB = 32
LANES = 128
TILES = WIDE // LANES
PARTS = 2
PART = WIDE // PARTS
PAD = 8


def gather(ring, part_of, store, sems):
    block, left, right, far, dev = ring
    send, recv, base = sems
    count = [base]

    def copy(src, dst, where):
        s = count[0]
        count[0] += 1
        return pltpu.make_async_remote_copy(
            src_ref=src, dst_ref=dst, send_sem=send.at[s], recv_sem=recv.at[s],
            device_id=where, device_id_type=MESH)

    def here(owner, part):
        return store.at[owner, :, pl.ds(part * PART, PART)]

    to_right, to_left, to_other = dev(1), dev(3), dev(0, True)
    out_r = [copy(part_of(c), here(block, c), to_right) for c in range(PARTS)]
    out_l = [copy(part_of(c), here(block, c), to_left) for c in range(PARTS)]
    own = [copy(part_of(c), here(block, c), to_other) for c in range(PARTS)]
    fwd_r = copy(here(left, 0), here(left, 0), to_right)
    fwd_l = copy(here(right, 1), here(right, 1), to_left)
    side_l = [copy(here(left, c), here(left, c), to_other) for c in range(PARTS)]
    side_r = [copy(here(right, c), here(right, c), to_other) for c in range(PARTS)]
    side_f = [copy(here(far, c), here(far, c), to_other) for c in range(PARTS)]
    return dict(out_r=out_r, out_l=out_l, own=own, fwd_r=fwd_r, fwd_l=fwd_l,
                side_l=side_l, side_r=side_r, side_f=side_f)


def relay(g, first, near, last):
    first()
    g["out_r"][0].wait_recv()
    g["fwd_r"].start()
    g["side_l"][0].start()
    g["out_l"][1].wait_recv()
    g["fwd_l"].start()
    g["side_r"][1].start()
    near[0]()
    g["out_r"][1].wait_recv()
    g["side_l"][1].start()
    g["out_l"][0].wait_recv()
    g["side_r"][0].start()
    near[1]()
    for c in range(PARTS):
        g["side_l"][c].wait_recv()
        g["side_r"][c].wait_recv()
    near[2]()
    g["fwd_r"].wait_recv()
    g["side_f"][0].start()
    g["fwd_l"].wait_recv()
    g["side_f"][1].start()
    last[0]()
    for c in range(PARTS):
        g["side_f"][c].wait_recv()
    last[1]()


def finish(g):
    for name in ("out_r", "out_l", "own", "side_l", "side_r", "side_f"):
        for c in g[name]:
            c.wait_send()
    g["fwd_r"].wait_send()
    g["fwd_l"].wait_send()


def kernel(tok, w_in, taps, residue, rate, w_out, out,
           win, wout, gat, mod, acc, total, gated, conv, gate0, decay, weight, entry_sub, ramp,
           tail_out, tail_in, state_out, state_in,
           w_sems, o_sems, own_sem, send1, recv1, send2, recv2, tail_send, tail_recv, st_send, st_recv):
    me = lax.axis_index("chan")
    ctx = lax.axis_index("ctx")
    x, core = me // 2, me % 2

    def at(step, flip=False):
        return lax.rem(x + step, 4) * 2 + (1 - core if flip else core)

    def dev(step, flip=False):
        return (ctx, at(step, flip))

    order = [me, at(0, True), at(3), at(1), at(3, True), at(1, True), at(2), at(2, True)]

    load_w = [pltpu.make_async_copy(w_in.at[:, b], win.at[:, b], w_sems.at[n]) for n, b in enumerate(order)]
    load_o = [pltpu.make_async_copy(w_out.at[b], wout.at[b], o_sems.at[n]) for n, b in enumerate(order)]
    load_t = pltpu.make_async_copy(tok, gat.at[me], own_sem)

    barrier = pltpu.get_barrier_semaphore()
    for d in (dev(1), dev(3), dev(0, True)):
        pl.semaphore_signal(barrier, inc=1, device_id=d, device_id_type=MESH)
    for back in range(1, CTX):
        @pl.when(ctx >= back)
        def _():
            pl.semaphore_signal(barrier, inc=1, device_id=(ctx - back, me), device_id_type=MESH)
    load_t.start()
    load_w[0].start()
    load_w[1].start()
    pl.semaphore_wait(barrier, 3 + CTX - 1 - ctx)

    ring = (me, at(3), at(1), at(2), dev)
    g1 = gather(ring, lambda c: tok.at[:, pl.ds(c * PART, PART)], gat, (send1, recv1, 0))
    g1["out_r"][0].start()
    g1["out_l"][1].start()
    g1["out_r"][1].start()
    g1["out_l"][0].start()
    for c in range(PARTS):
        g1["own"][c].start()
    for n in range(2, BLOCKS):
        load_w[n].start()
    for n in range(BLOCKS):
        load_o[n].start()

    dec = jnp.exp(-rate[...])
    decay[0] = dec
    for n, power in enumerate((8, 32, 64, 128, 256)):
        decay[n + 1] = jnp.exp(-rate[...] * float(power))
    weight[...] = residue[...] * jnp.sqrt(1.0 - jnp.exp(-2.0 * rate[...]))
    steps = lax.broadcasted_iota(jnp.int32, (8, WIDE), 0).astype(F32) + 1.0
    for r in range(MODES):
        ramp[r] = jnp.exp(-rate[r:r + 1] * steps) * weight[r:r + 1]

    def project(n, fresh=False, slots=(0, 1, 2)):
        b = order[n]
        load_w[n].wait()
        for s in slots:
            part = jnp.dot(gat[b], win[s, b], preferred_element_type=F32)
            if fresh:
                acc[s, PAD:PAD + ROWS] = part
            else:
                acc[s, PAD:PAD + ROWS] += part

    def do_first():
        load_t.wait()
        project(0, True)

    def do_sibling():
        for c in range(PARTS):
            g1["own"][c].wait_recv()
        project(1)

    def do_near():
        project(2)
        project(3)

    def do_near_other():
        project(4)
        project(5)

    relay(g1, do_first, (do_sibling, do_near, do_near_other),
          (lambda: project(6), lambda: project(7)))

    for s in range(3):
        tail_out[2 * s:2 * s + 2] = acc[s, PAD + ROWS - 2:PAD + ROWS].astype(BF16).astype(F32)
    tail = pltpu.make_async_remote_copy(
        src_ref=tail_out, dst_ref=tail_in, send_sem=tail_send.at[0], recv_sem=tail_recv.at[0],
        device_id=(lax.rem(ctx + 1, CTX), me), device_id_type=MESH)

    @pl.when(ctx < CTX - 1)
    def _():
        tail.start()

    for s in range(3):
        for q in range(8):
            rows = slice(PAD + SUB * q, PAD + SUB * (q + 1))
            acc[s, rows] = acc[s, rows].astype(BF16).astype(F32)

    @pl.when(ctx > 0)
    def _():
        tail.wait_recv()
        for s in range(3):
            acc[s, PAD - 2:PAD] = tail_in[2 * s:2 * s + 2]

    @pl.when(ctx == 0)
    def _():
        for s in range(3):
            acc[s, PAD - 2:PAD] = jnp.zeros((2, WIDE), F32)

    def filtered(s, q):
        value = None
        for tap in range(SHORT):
            first = PAD + SUB * q - tap
            term = taps[tap, s:s + 1] * acc[s, first:first + SUB]
            value = term if value is None else value + term
        return value

    def split(ref, q, value):
        for tile in range(TILES):
            ref[tile, SUB * q:SUB * (q + 1)] = value[:, tile * LANES:(tile + 1) * LANES]

    for q in range(8):
        split(gated, q, (filtered(1, q) * filtered(2, q)).astype(BF16).astype(F32))

    row = lax.broadcasted_iota(jnp.int32, (8, LANES), 0)

    def spread(ref, r, lanes):
        return jnp.broadcast_to(ref[r:r + 1, lanes], (8, LANES))

    @pl.loop(0, TILES)
    def _(tile):
        lanes = pl.ds(pl.multiple_of(tile * LANES, LANES), LANES)
        d = [spread(decay.at[0], r, lanes) for r in range(MODES)]

        def step(j, states):
            g = gated[tile, pl.ds(j, 8, stride=SUB)]
            return tuple(d[r] * states[r] + g for r in range(MODES))

        states = lax.fori_loop(0, SUB, step, tuple(jnp.zeros((8, LANES), F32) for _ in range(MODES)), unroll=4)
        for r in range(MODES):
            s = states[r]
            for n, shift in enumerate((1, 2, 4)):
                s = s + jnp.where(row >= shift, spread(decay.at[2 + n], r, lanes) * pltpu.roll(s, shift, 0), 0.0)
            state_out[r:r + 1, lanes] = s[7:8]
            entry_sub[r, :, lanes] = jnp.where(row >= 1, pltpu.roll(s, 1, 0), 0.0)

    for ahead in range(1, CTX):
        @pl.when(ctx + ahead < CTX)
        def _():
            pltpu.make_async_remote_copy(
                src_ref=state_out, dst_ref=state_in.at[ctx], send_sem=st_send.at[ahead], recv_sem=st_recv.at[ctx],
                device_id=(lax.rem(ctx + ahead, CTX), me), device_id_type=MESH).start()

    for q in range(8):
        split(gate0, q, filtered(0, q))

    @pl.loop(0, TILES)
    def _(tile):
        lanes = pl.ds(pl.multiple_of(tile * LANES, LANES), LANES)
        d = [spread(decay.at[0], r, lanes) for r in range(MODES)]
        w = [spread(weight, r, lanes) for r in range(MODES)]

        def step(j, states):
            g = gated[tile, pl.ds(j, 8, stride=SUB)]
            states = tuple(d[r] * states[r] + g for r in range(MODES))
            terms = [w[r] * states[r] for r in range(MODES)]
            while len(terms) > 1:
                terms = [a + b for a, b in zip(terms[::2], terms[1::2])]
            conv[tile, pl.ds(j, 8, stride=SUB)] = terms[0]
            return states

        lax.fori_loop(0, SUB, step, tuple(entry_sub[r, :, lanes] for r in range(MODES)), unroll=2)

    def merge(j, entry):
        pltpu.make_async_remote_copy(
            src_ref=state_out, dst_ref=state_in.at[j], send_sem=st_send.at[0], recv_sem=st_recv.at[j],
            device_id=(ctx, me), device_id_type=MESH).wait_recv()
        return decay[5] * entry + state_in[j]

    entry = lax.fori_loop(0, ctx, merge, jnp.zeros((MODES, WIDE), F32))
    state_in[CTX - 1] = entry

    def modulate(part):
        @pl.loop(part * PART // LANES, (part + 1) * PART // LANES)
        def _(tile):
            lanes = pl.ds(pl.multiple_of(tile * LANES, LANES), LANES)
            z = tuple(ramp[r, :, lanes] * state_in[CTX - 1, r:r + 1, lanes] for r in range(MODES))
            d8 = [spread(decay.at[1], r, lanes) for r in range(MODES)]

            def step(q, z):
                halves = []
                for half in range(2):
                    rows = pl.ds(pl.multiple_of(q * 16 + half * 8, 8), 8)
                    terms = list(z)
                    while len(terms) > 1:
                        terms = [a + b for a, b in zip(terms[::2], terms[1::2])]
                    halves.append(gate0[tile, rows] * (conv[tile, rows] + terms[0]))
                    z = tuple(d8[r] * z[r] for r in range(MODES))
                mod[me, pl.ds(pl.multiple_of(q * 16, 16), 16), lanes] = jnp.concatenate(halves, 0).astype(BF16)
                return z

            lax.fori_loop(0, ROWS // 16, step, z)

    g2 = gather(ring, lambda c: mod.at[me, :, pl.ds(c * PART, PART)], mod, (send2, recv2, 0))
    modulate(0)
    g2["out_r"][0].start()
    modulate(1)
    g2["out_l"][1].start()
    g2["out_r"][1].start()
    g2["out_l"][0].start()
    for c in range(PARTS):
        g2["own"][c].start()

    def mix(n, fresh=False):
        b = order[n]
        load_o[n].wait()
        part = jnp.dot(mod[b], wout[b], preferred_element_type=F32)
        if fresh:
            total[...] = part
        else:
            total[...] += part

    def mix_sibling():
        for c in range(PARTS):
            g2["own"][c].wait_recv()
        mix(1)

    def mix_near():
        mix(2)
        mix(3)

    def mix_near_other():
        mix(4)
        mix(5)

    def mix_last():
        b = order[7]
        load_o[7].wait()
        out[...] = (total[...] + jnp.dot(mod[b], wout[b], preferred_element_type=F32)).astype(BF16)

    relay(g2, lambda: mix(0, True), (mix_sibling, mix_near, mix_near_other), (lambda: mix(6), mix_last))

    finish(g1)
    finish(g2)

    @pl.when(ctx < CTX - 1)
    def _():
        tail.wait_send()

    for ahead in range(1, CTX):
        @pl.when(ctx + ahead < CTX)
        def _():
            pltpu.make_async_remote_copy(
                src_ref=state_out, dst_ref=state_in.at[ctx], send_sem=st_send.at[ahead], recv_sem=st_recv.at[ctx],
                device_id=(lax.rem(ctx + ahead, CTX), me), device_id_type=MESH).wait_send()


def per_device(tokens, w_in, short_kernel, residue, rate, w_out):
    w_in = jnp.transpose(w_in, (1, 0, 2)).reshape(3, BLOCKS, WIDE, WIDE)
    w_out = w_out.reshape(BLOCKS, WIDE, WIDE)
    vmem = pl.BlockSpec(memory_space=pltpu.VMEM)
    hbm = pl.BlockSpec(memory_space=pl.ANY)
    dma = pltpu.SemaphoreType.DMA
    return pl.pallas_call(
        kernel,
        out_shape=jax.ShapeDtypeStruct((ROWS, WIDE), BF16),
        in_specs=[hbm, hbm, vmem, vmem, vmem, hbm],
        out_specs=vmem,
        scratch_shapes=[
            pltpu.VMEM((3, BLOCKS, WIDE, WIDE), BF16),
            pltpu.VMEM((BLOCKS, WIDE, WIDE), BF16),
            pltpu.VMEM((BLOCKS, ROWS, WIDE), BF16),
            pltpu.VMEM((BLOCKS, ROWS, WIDE), BF16),
            pltpu.VMEM((3, PAD + ROWS, WIDE), F32),
            pltpu.VMEM((ROWS, WIDE), F32),
            pltpu.VMEM((TILES, ROWS + SUB, LANES), F32),
            pltpu.VMEM((TILES, ROWS + SUB, LANES), F32),
            pltpu.VMEM((TILES, ROWS, LANES), F32),
            pltpu.VMEM((6, MODES, WIDE), F32),
            pltpu.VMEM((MODES, WIDE), F32),
            pltpu.VMEM((MODES, 8, WIDE), F32),
            pltpu.VMEM((MODES, 8, WIDE), F32),
            pltpu.VMEM((8, WIDE), F32),
            pltpu.VMEM((8, WIDE), F32),
            pltpu.VMEM((MODES, WIDE), F32),
            pltpu.VMEM((CTX, MODES, WIDE), F32),
            dma((BLOCKS,)), dma((BLOCKS,)), dma,
            dma((16,)), dma((16,)), dma((16,)), dma((16,)),
            dma((1,)), dma((1,)), dma((CTX,)), dma((CTX,)),
        ],
        compiler_params=pltpu.CompilerParams(
            collective_id=0, has_side_effects=True, vmem_limit_bytes=48 * 2**20),
        cost_estimate=pl.CostEstimate(
            flops=2 * ROWS * 4096 * 2048, bytes_accessed=17 * 2**20, transcendentals=0),
    )(tokens, w_in, short_kernel, residue.T, rate.T, w_out)


def solution(mesh):
    in_specs = (
        P("ctx", "chan"),
        P(None, None, "chan"),
        P(None, None, "chan"),
        P("chan", None),
        P("chan", None),
        P(None, "chan"),
    )
    return jax.shard_map(
        per_device, mesh=mesh, in_specs=in_specs, out_specs=P("ctx", "chan"), check_vma=False)
```

time: 451 us -> 50.6 us (0.11)
  waiting for transfers between devices: 159 us -> 0 us
  matrix products: 131 us -> 0 us
  local copies, waits for them, and re-layouts: 87.4 us -> 6.09 us
  Pallas kernels: 0 us -> 44.1 us
  starting transfers between devices: 33.3 us -> 0 us
  other arithmetic: 22.7 us -> 0 us
  between operations: 13.6 us -> 0.01 us
    dot_general x20 -> x0, matrix products: 131 us -> none  [the longest x16 92.4 us: sub_states(): jnp.einsum('ckj,cjr->ckr', pieces, tail_power, precision=exact)]
    ppermute x16 -> x0, waiting for transfers between devices: 117 us -> none  [shifted(): return lax.ppermute(value, axis, pairs)]
    pallas_call x0 -> x1, Pallas kernels: none -> 44.1 us  [per_device(): pl.pallas_call(kernel, out_shape=jax.ShapeDtypeStruct((ROWS, WIDE), BF16)...]
    all_gather x2 -> x0, waiting for transfers between devices: 41.5 us -> none  [the longest x1 40.6 us: per_device(): lax.all_gather(modulated, 'chan', axis=1, tiled=True)]
    ppermute x16 -> x0, starting transfers between devices: 33.2 us -> none  [shifted(): return lax.ppermute(value, axis, pairs)]
    gather x2 -> x0, local copies, waits for them, and re-layouts: 33 us -> none  [per_device(): impulse_rows[:, jnp.clip(lagged, 0, sub - 1)]]
    unnamed x21 -> x11, local copies, waits for them, and re-layouts: 18 us -> 6.09 us
    while x16 -> x0, local copies, waits for them, and re-layouts: 10.7 us -> none
  transfers between devices with their start and end apart: 18 -> 0, of which waited for: 17 -> 0; matrix products, arithmetic and copies ran while one was open for 16% -> 0% of each run, Pallas kernels for 0% -> 0%
where the time goes in v1:
time: 50.6 us; the launch traced here: 50.3 us
  Pallas kernels  44.1 us (87%)
  local copies, waits for them, and re-layouts  6.09 us (12%)
    pallas_call x1, Pallas kernels, per_device(): pl.pallas_call(kernel, out_shape=jax.ShapeDtypeStruct((ROWS, WIDE), BF16)...  44.1 us
    unnamed x11, local copies, waits for them, and re-layouts  6.09 us

profile of v1, /device:TPU:25, one launch (start us, length us, event | category | flops | bytes accessed | tf_op | source)
XLA Modules:
  0.0 50.3 jit_solution(17196475839382269782)
XLA Ops:
  0.0 0.0 copy-start
  0.0 2.2 %copy-done = bf16[4096,512]{1,0:T(8,128)(2,1)S(1)} copy-done((bf16[4096,512]{1,0:T(8,128)(2,1)S(1)}, bf16[4096,512]{1,0:T(8,128)(2,1)}, u32[]{:S(2)}) %copy-start) | copy-done | bytes 4194328
  2.2 0.0 copy-start.1
  2.2 0.9 %copy-done.1 = bf16[256,512]{1,0:T(8,128)(2,1)S(1)} copy-done((bf16[256,512]{1,0:T(8,128)(2,1)S(1)}, bf16[256,512]{1,0:T(8,128)(2,1)}, u32[]{:S(2)}) %copy-start.1) | copy-done | bytes 262168
  3.1 0.0 copy-start.2
  3.1 0.8 %copy-done.2 = f32[512,16]{0,1:T(8,128)S(1)} copy-done((f32[512,16]{0,1:T(8,128)S(1)}, f32[512,16]{0,1:T(8,128)}, u32[]{:S(2)}) %copy-start.2) | copy-done | bytes 32792
  3.9 0.0 copy-start.3
  3.9 0.8 %copy-done.3 = f32[512,16]{0,1:T(8,128)S(1)} copy-done((f32[512,16]{0,1:T(8,128)S(1)}, f32[512,16]{0,1:T(8,128)}, u32[]{:S(2)}) %copy-start.3) | copy-done | bytes 32792
  4.7 0.0 copy-start.4
  4.7 0.7 %copy-done.4 = f32[3,3,512]{2,1,0:T(4,128)S(1)} copy-done((f32[3,3,512]{2,1,0:T(4,128)S(1)}, f32[3,3,512]{2,1,0:T(4,128)}, u32[]{:S(2)}) %copy-start.4) | copy-done | bytes 18456
  5.4 44.1 %shard_map.64 = bf16[256,512]{1,0:T(8,128)(2,1)S(1)} custom-call(bf16[256,512]{1,0:T(8,128)(2,1)S(1)} %copy-done.1, bf16[3,8,512,512]{3,2,1,0:T(8,128)(2,1)} %bitcast.9, f32[3,3,512]{2,1,0:T(4,128)S(1)} %copy-done.4, f32[16,512]{1,0:T(8,128)S(1)} %bitcast.7, f32[16,512]{1,0:T(8,128)S(1)} %bitcast.8, bf16[8,512,512]{2,1,0:T(8,128)(2,1)S(1)} %bitcast.6), custom_call_target="tpu_custom_call" | custom-call | flops 4294967296 | bytes 17825792 | tf_op jit(solution)/shard_map/pallas_call | solution.py:355
  49.5 0.7 %copy.8 = bf16[256,512]{1,0:T(8,128)(2,1)} copy(bf16[256,512]{1,0:T(8,128)(2,1)S(1)} %shard_map.64) | data formatting | bytes 524288
Async XLA Ops:
  0.0 2.2 %copy-start = (bf16[4096,512]{1,0:T(8,128)(2,1)S(1)}, bf16[4096,512]{1,0:T(8,128)(2,1)}, u32[]{:S(2)}) copy-start(bf16[4096,512]{1,0:T(8,128)(2,1)} %param.11) | copy-start | bytes 12582916
  2.2 0.9 %copy-start.1 = (bf16[256,512]{1,0:T(8,128)(2,1)S(1)}, bf16[256,512]{1,0:T(8,128)(2,1)}, u32[]{:S(2)}) copy-start(bf16[256,512]{1,0:T(8,128)(2,1)} %tok.1) | copy-start | bytes 786436
  3.1 0.8 %copy-start.2 = (f32[512,16]{0,1:T(8,128)S(1)}, f32[512,16]{0,1:T(8,128)}, u32[]{:S(2)}) copy-start(f32[512,16]{0,1:T(8,128)} %param.9) | copy-start | bytes 98308
  3.9 0.8 %copy-start.3 = (f32[512,16]{0,1:T(8,128)S(1)}, f32[512,16]{0,1:T(8,128)}, u32[]{:S(2)}) copy-start(f32[512,16]{0,1:T(8,128)} %param.10) | copy-start | bytes 98308
  4.7 0.7 %copy-start.4 = (f32[3,3,512]{2,1,0:T(4,128)S(1)}, f32[3,3,512]{2,1,0:T(4,128)}, u32[]{:S(2)}) copy-start(f32[3,3,512]{2,1,0:T(4,128)} %taps.1) | copy-start | bytes 55300

commit v2 on v0

v2 whole, which is shorter than its diff:
```python
import jax
import jax.numpy as jnp
from jax import lax
from jax.experimental import pallas as pl
from jax.experimental.pallas import tpu as pltpu
from jax.sharding import PartitionSpec as P

MESH = pl.DeviceIdType.MESH
F32 = jnp.float32
BF16 = jnp.bfloat16
STATE = jnp.float32
CTX = 16
ROWS = 256
WIDE = 512
BLOCKS = 8
MODES = 16
SHORT = 3
RUNS = 8
SUB = ROWS // RUNS
LANES = 128
TILES = WIDE // LANES
HALF = WIDE // 2
TALL = ROWS // 2
HEAD = 16


def remote(src, dst, send, recv, where):
    return pltpu.make_async_remote_copy(
        src_ref=src, dst_ref=dst, send_sem=send, recv_sem=recv, device_id=where, device_id_type=MESH)


class Gather:
    def __init__(self, source, store, top, block, left, right, far, dev, send, recv):
        count = [0]

        def copy(src, dst, where):
            s = count[0]
            count[0] += 1
            return remote(src, dst, send.at[s], recv.at[s], where)

        def here(owner, c, h):
            return store.at[owner, pl.ds(top + h * TALL, TALL), pl.ds(c * HALF, HALF)]

        quarters = [(c, h) for c in range(2) for h in range(2)]
        to_right, to_left, to_other = dev(1), dev(3), dev(0, True)
        self.right = {q: copy(source(*q), here(block, *q), to_right) for q in quarters}
        self.left = {q: copy(source(*q), here(block, *q), to_left) for q in quarters}
        self.own = {q: copy(source(*q), here(block, *q), to_other) for q in quarters}
        self.on_right = [copy(here(left, c, 0), here(left, c, 0), to_right) for c in range(2)]
        self.on_left = [copy(here(right, c, 1), here(right, c, 1), to_left) for c in range(2)]
        self.side_l = {q: copy(here(left, *q), here(left, *q), to_other) for q in quarters}
        self.side_r = {q: copy(here(right, *q), here(right, *q), to_other) for q in quarters}
        self.side_f = {q: copy(here(far, *q), here(far, *q), to_other) for q in quarters}

    def begin(self, c):
        for h in range(2):
            self.right[c, h].start()
            self.left[c, 1 - h].start()
        for h in range(2):
            self.own[c, h].start()

    def relay(self, work):
        work[0]()
        for c in range(2):
            self.right[c, 0].wait_recv()
            self.on_right[c].start()
            self.side_l[c, 0].start()
            self.left[c, 1].wait_recv()
            self.on_left[c].start()
            self.side_r[c, 1].start()
            work[1 + 2 * c]()
            self.right[c, 1].wait_recv()
            self.side_l[c, 1].start()
            self.left[c, 0].wait_recv()
            self.side_r[c, 0].start()
            work[2 + 2 * c]()
        for c in range(2):
            self.on_right[c].wait_recv()
            self.side_f[c, 0].start()
            self.on_left[c].wait_recv()
            self.side_f[c, 1].start()
            work[5 + c]()

    def wait_side(self, sides, c):
        for side in sides:
            for h in range(2):
                side[c, h].wait_recv()

    def finish(self):
        for group in (self.right, self.left, self.own, self.side_l, self.side_r, self.side_f):
            for c in group.values():
                c.wait_send()
        for c in self.on_right + self.on_left:
            c.wait_send()


def total_of(terms):
    while len(terms) > 1:
        terms = [a + b for a, b in zip(terms[::2], terms[1::2])]
    return terms[0]


def kernel(tok, w_in, taps_hbm, residue_hbm, rate_hbm, w_out, out,
           taps, residue, rate, win, wout, gat, mod, acc, total, gated, conv, gate0,
           decay, weight, run_state, run_decay, ramp, halo_out, halo_in, state_out, state_in, entry,
           w_sems, o_sems, own_sem, small_sems, send1, recv1, send2, recv2, halo_send, halo_recv,
           state_send, state_recv, ready, next_in, later_in):
    me = lax.axis_index("chan")
    ctx = lax.axis_index("ctx")
    x, core = me // 2, me % 2

    def at(step, flip=False):
        return lax.rem(x + step, 4) * 2 + (1 - core if flip else core)

    def dev(step, flip=False):
        return (ctx, at(step, flip))

    order = [me, at(0, True), at(3), at(1), at(3, True), at(1, True), at(2), at(2, True)]

    load_w = [pltpu.make_async_copy(w_in.at[:, b], win.at[:, b], w_sems.at[n]) for n, b in enumerate(order)]
    load_o = [pltpu.make_async_copy(w_out.at[b], wout.at[b], o_sems.at[n]) for n, b in enumerate(order)]
    load_t = pltpu.make_async_copy(tok, gat.at[me, pl.ds(HEAD, ROWS)], own_sem)
    load_s = [pltpu.make_async_copy(src, dst, small_sems.at[n]) for n, (src, dst) in enumerate(
        ((rate_hbm, rate), (residue_hbm, residue), (taps_hbm, taps)))]

    barrier = pltpu.get_barrier_semaphore()

    def greet(sem, where):
        pl.semaphore_signal(sem, inc=1, device_id=where, device_id_type=MESH)

    def chip(step, of_core):
        return (ctx, lax.rem(x + step, 4) * 2 + of_core)

    load_t.start()
    for c in load_s:
        c.start()

    @pl.when(core == 0)
    def _():
        greet(barrier, chip(1, 0))
        greet(barrier, chip(3, 0))
        pl.semaphore_wait(barrier, 5)
        for step in (0, 1, 3):
            greet(ready, chip(step, 1))

    @pl.when(core == 1)
    def _():
        for step in (0, 1, 3):
            greet(barrier, chip(step, 0))
        pl.semaphore_wait(ready, 3)

    ring = (me, at(3), at(1), at(2), dev)
    g1 = Gather(lambda c, h: tok.at[pl.ds(h * TALL, TALL), pl.ds(c * HALF, HALF)], gat, HEAD, *ring, send1, recv1)
    g1.begin(0)
    g1.begin(1)

    even = lax.rem(x, 2) == 0

    @pl.when((core == 1) & even & (ctx > 0))
    def _():
        greet(barrier, (ctx - 1, me))

    for back in range(1, CTX):
        @pl.when((core == 1) & jnp.logical_not(even) & (ctx >= back))
        def _():
            greet(barrier, (ctx - back, me))

    load_w[0].start()
    load_w[1].start()
    load_t.wait()
    row16 = lax.broadcasted_iota(jnp.int32, (HEAD, LANES), 0)
    packed = jnp.zeros((HEAD, LANES), F32)
    for t in range(TILES):
        last = gat[me, ROWS:ROWS + HEAD, t * LANES:(t + 1) * LANES].astype(F32)
        packed = jnp.where(row16 // 2 == t, pltpu.roll(last, 2 * t + 2, 0), packed)
    halo_out[...] = packed.astype(BF16)
    halos = [remote(halo_out, halo_in.at[me], halo_send.at[o], halo_recv.at[me],
                    (lax.rem(ctx + 1, CTX), lax.rem(me + o, BLOCKS))) for o in range(BLOCKS)]

    for n in range(2, BLOCKS):
        load_w[n].start()
    for n in range(BLOCKS):
        load_o[n].start()
    for c in load_s:
        c.wait()

    decay[0] = jnp.exp(-rate[...])
    for n, power in enumerate((8, 32, 64, 128, 256)):
        decay[n + 1] = jnp.exp(-rate[...] * float(power))
    weight[...] = residue[...] * jnp.sqrt(1.0 - jnp.exp(-2.0 * rate[...]))
    sublane = lax.broadcasted_iota(jnp.int32, (8, WIDE), 0).astype(F32)
    for r in range(MODES):
        ramp[r] = jnp.exp(-rate[r:r + 1] * (sublane + 1.0)) * weight[r:r + 1]
        run_decay[r] = jnp.exp(-rate[r:r + 1] * (float(SUB) * (float(RUNS - 1) - sublane)))

    def project(n, part=None, fresh=False, slots=(0, 1, 2), last=False):
        b = order[n]
        cols = slice(0, WIDE) if part is None else slice(part * HALF, (part + 1) * HALF)
        for s in slots:
            value = jnp.dot(gat[b, :, cols], win[s, b, cols], preferred_element_type=F32)
            if not fresh:
                value = acc[s] + value
            if last:
                value = value.astype(BF16).astype(F32)
            acc[s] = value

    def take_halo():
        @pl.when(ctx > 0)
        def _():
            for q in range(BLOCKS):
                remote(halo_out, halo_in.at[q], halo_send.at[0], halo_recv.at[q], dev(1)).wait_recv()
                rows = halo_in[q].astype(F32)
                for t in range(TILES):
                    gat[q, 0:HEAD, t * LANES:(t + 1) * LANES] = pltpu.roll(rows, HEAD - 2 - 2 * t, 0).astype(BF16)

        @pl.when(ctx == 0)
        def _():
            for q in range(BLOCKS):
                gat[q, 0:HEAD] = jnp.zeros((HEAD, WIDE), BF16)

    def project_own():
        load_w[0].wait()
        project(0, fresh=True)

    def project_other():
        load_w[1].wait()
        for c in range(2):
            g1.wait_side([g1.own], c)
        project(1)

    def project_near():
        load_w[2].wait()
        project(2)
        load_w[3].wait()
        project(3)

    def project_near_other():
        for c in range(2):
            g1.wait_side([g1.side_l, g1.side_r], c)
        load_w[4].wait()
        project(4)

    def project_far():
        load_w[5].wait()
        project(5)
        load_w[6].wait()
        project(6, 0)
        load_w[7].wait()
        g1.wait_side([g1.side_f], 0)
        project(7, 0)
        project(6, 1)
        g1.wait_side([g1.side_f], 1)
        project(7, 1, slots=(1, 2), last=True)

    def hear_next():
        @pl.when((ctx < CTX - 1) & (core == 1) & even)
        def _():
            pl.semaphore_wait(barrier, 1)
            for where in (chip(0, 0), chip(1, 0), chip(1, 1)):
                greet(next_in, where)

    def send_halo():
        @pl.when((ctx < CTX - 1) & jnp.logical_not((core == 1) & even))
        def _():
            pl.semaphore_wait(next_in, 1)

        @pl.when(ctx < CTX - 1)
        def _():
            for c in halos:
                c.start()

    def hear_later():
        @pl.when((ctx < CTX - 1) & (core == 1) & jnp.logical_not(even))
        def _():
            pl.semaphore_wait(barrier, CTX - 1 - ctx)
            for where in (chip(0, 0), chip(3, 0), chip(3, 1)):
                greet(later_in, where)

    def idle():
        pass

    def project_first():
        take_halo()
        project_own()
        project_other()

    def project_middle():
        hear_later()
        project_near()
        project_near_other()

    g1.relay((hear_next, send_halo, idle, idle, project_first, project_middle, project_far))

    def filtered(s, q, lanes):
        value = None
        for tap in range(SHORT):
            first = HEAD + SUB * q - tap
            term = taps[tap, s:s + 1, lanes] * acc[s, first:first + SUB, lanes]
            value = term if value is None else value + term
        return value

    row = lax.broadcasted_iota(jnp.int32, (8, LANES), 0)

    def spread(ref, r, lanes):
        return jnp.broadcast_to(ref[r:r + 1, lanes], (8, LANES))

    def lanes_of(tile):
        return pl.ds(pl.multiple_of(tile * LANES, LANES), LANES)

    def block_state(half):
        for t in range(2 * half, 2 * half + 2):
            lanes = slice(t * LANES, (t + 1) * LANES)
            for q in range(RUNS):
                gated[t, SUB * q:SUB * (q + 1)] = (
                    filtered(1, q, lanes) * filtered(2, q, lanes)).astype(BF16).astype(F32)

        @pl.loop(2 * half, 2 * half + 2)
        def _(tile):
            lanes = lanes_of(tile)
            d = [spread(decay.at[0], r, lanes) for r in range(MODES)]

            def step(j, states):
                g = gated[tile, pl.ds(j, RUNS, stride=SUB)]
                return tuple(d[r] * states[r] + g for r in range(MODES))

            states = lax.fori_loop(0, SUB, step, tuple(jnp.zeros((8, LANES), F32) for _ in range(MODES)), unroll=8)
            where = pl.ds(pl.multiple_of((tile - 2 * half) * LANES, LANES), LANES)
            for r in range(MODES):
                run_state[r, :, lanes] = states[r]
                state_out[half, r:r + 1, where] = jnp.sum(
                    run_decay[r, :, lanes] * states[r], axis=0, keepdims=True).astype(STATE)

        if half == 0:
            @pl.when((ctx < CTX - 1) & jnp.logical_not((core == 1) & jnp.logical_not(even)))
            def _():
                pl.semaphore_wait(later_in, 1)

        for ahead in range(1, CTX):
            @pl.when(ctx + ahead < CTX)
            def _():
                remote(state_out.at[half], state_in.at[half, ctx], state_send.at[half, ahead], state_recv.at[half, ctx],
                       (lax.rem(ctx + ahead, CTX), me)).start()

    block_state(0)
    block_state(1)
    project(7, 1, slots=(0,), last=True)

    def own_part(half):
        for t in range(2 * half, 2 * half + 2):
            lanes = slice(t * LANES, (t + 1) * LANES)
            for q in range(RUNS):
                gate0[t, SUB * q:SUB * (q + 1)] = filtered(0, q, lanes)

        @pl.loop(2 * half, 2 * half + 2)
        def _(tile):
            lanes = lanes_of(tile)
            before = []
            for r in range(MODES):
                s = run_state[r, :, lanes]
                for n, shift in enumerate((1, 2, 4)):
                    s = s + jnp.where(row >= shift, spread(decay.at[2 + n], r, lanes) * pltpu.roll(s, shift, 0), 0.0)
                before.append(jnp.where(row >= 1, pltpu.roll(s, 1, 0), 0.0))
            d = [spread(decay.at[0], r, lanes) for r in range(MODES)]
            w = [spread(weight, r, lanes) for r in range(MODES)]

            def step(j, states):
                g = gated[tile, pl.ds(j, RUNS, stride=SUB)]
                sums = [None] * 4
                after = []
                for r in range(MODES):
                    s = d[r] * states[r] + g
                    after.append(s)
                    term = w[r] * s
                    sums[r % 4] = term if sums[r % 4] is None else sums[r % 4] + term
                conv[tile, pl.ds(j, RUNS, stride=SUB)] = total_of(sums)
                return tuple(after)

            lax.fori_loop(0, SUB, step, tuple(before), unroll=2)

    own_part(0)
    own_part(1)

    def merge(half):
        def add(j, value):
            remote(state_out.at[half], state_in.at[half, j], state_send.at[half, 0], state_recv.at[half, j],
                   dev(1)).wait_recv()
            return decay[5, :, half * HALF:(half + 1) * HALF] * value + state_in[half, j].astype(F32)

        entry[:, half * HALF:(half + 1) * HALF] = lax.fori_loop(0, ctx, add, jnp.zeros((MODES, HALF), F32))

    def modulate(half):
        @pl.loop(2 * half, 2 * half + 2)
        def _(tile):
            lanes = lanes_of(tile)
            z = tuple(ramp[r, :, lanes] * entry[r:r + 1, lanes] for r in range(MODES))
            d8 = [spread(decay.at[1], r, lanes) for r in range(MODES)]

            def step(q, z):
                halves = []
                for part in range(2):
                    rows = pl.ds(pl.multiple_of(q * 16 + part * 8, 8), 8)
                    halves.append(gate0[tile, rows] * (conv[tile, rows] + total_of(list(z))))
                    z = tuple(d8[r] * z[r] for r in range(MODES))
                mod[me, pl.ds(pl.multiple_of(q * 16, 16), 16), lanes] = jnp.concatenate(halves, 0).astype(BF16)
                return z

            lax.fori_loop(0, ROWS // 16, step, z, unroll=2)

    g2 = Gather(lambda c, h: mod.at[me, pl.ds(h * TALL, TALL), pl.ds(c * HALF, HALF)], mod, 0, *ring, send2, recv2)
    for half in range(2):
        merge(half)
        modulate(half)
        g2.begin(half)

    def mix(n, part=None, fresh=False):
        b = order[n]
        cols = slice(0, WIDE) if part is None else slice(part * HALF, (part + 1) * HALF)
        value = jnp.dot(mod[b, :, cols], wout[b, cols], preferred_element_type=F32)
        total[...] = value if fresh else total[...] + value

    def mix_own():
        for c in load_o:
            c.wait()
        mix(0, fresh=True)

    def mix_other():
        for c in range(2):
            g2.wait_side([g2.own], c)
        mix(1)

    def mix_near():
        mix(2)
        mix(3)

    def mix_near_other():
        for c in range(2):
            g2.wait_side([g2.side_l, g2.side_r], c)
        mix(4)
        mix(5)
        mix(6, 0)

    def mix_far():
        g2.wait_side([g2.side_f], 0)
        mix(7, 0)
        mix(6, 1)
        g2.wait_side([g2.side_f], 1)
        b = order[7]
        out[...] = (total[...] + jnp.dot(
            mod[b, :, HALF:], wout[b, HALF:], preferred_element_type=F32)).astype(BF16)

    g2.relay((idle, mix_own, mix_other, idle, mix_near, mix_near_other, mix_far))

    g1.finish()
    g2.finish()

    @pl.when(ctx < CTX - 1)
    def _():
        for c in halos:
            c.wait_send()

    for half in range(2):
        for ahead in range(1, CTX):
            @pl.when(ctx + ahead < CTX)
            def _():
                remote(state_out.at[half], state_in.at[half, ctx], state_send.at[half, ahead],
                       state_recv.at[half, ctx], (lax.rem(ctx + ahead, CTX), me)).wait_send()


def per_device(tokens, w_in, short_kernel, residue, rate, w_out):
    w_in = jnp.transpose(w_in, (1, 0, 2)).reshape(3, BLOCKS, WIDE, WIDE)
    w_out = w_out.reshape(BLOCKS, WIDE, WIDE)
    dma = pltpu.SemaphoreType.DMA
    vmem = pltpu.VMEM
    return pl.pallas_call(
        kernel,
        out_shape=jax.ShapeDtypeStruct((ROWS, WIDE), BF16),
        in_specs=[pl.BlockSpec(memory_space=pltpu.HBM)] * 6,
        out_specs=pl.BlockSpec(memory_space=pltpu.VMEM),
        scratch_shapes=[
            vmem((SHORT, 3, WIDE), F32),
            vmem((MODES, WIDE), F32),
            vmem((MODES, WIDE), F32),
            vmem((3, BLOCKS, WIDE, WIDE), BF16),
            vmem((BLOCKS, WIDE, WIDE), BF16),
            vmem((BLOCKS, HEAD + ROWS, WIDE), BF16),
            vmem((BLOCKS, ROWS, WIDE), BF16),
            vmem((3, HEAD + ROWS, WIDE), F32),
            vmem((ROWS, WIDE), F32),
            vmem((TILES, ROWS + SUB, LANES), F32),
            vmem((TILES, ROWS + SUB, LANES), F32),
            vmem((TILES, ROWS, LANES), F32),
            vmem((6, MODES, WIDE), F32),
            vmem((MODES, WIDE), F32),
            vmem((MODES, 8, WIDE), F32),
            vmem((MODES, 8, WIDE), F32),
            vmem((MODES, 8, WIDE), F32),
            vmem((HEAD, LANES), BF16),
            vmem((BLOCKS, HEAD, LANES), BF16),
            vmem((2, MODES, HALF), STATE),
            vmem((2, CTX, MODES, HALF), STATE),
            vmem((MODES, WIDE), F32),
            dma((BLOCKS,)), dma((BLOCKS,)), dma, dma((3,)),
            dma((32,)), dma((32,)), dma((32,)), dma((32,)),
            dma((BLOCKS,)), dma((BLOCKS,)),
            dma((2, CTX)), dma((2, CTX)),
            pltpu.SemaphoreType.REGULAR, pltpu.SemaphoreType.REGULAR, pltpu.SemaphoreType.REGULAR,
        ],
        compiler_params=pltpu.CompilerParams(
            collective_id=0, has_side_effects=True, vmem_limit_bytes=60 * 2**20),
        cost_estimate=pl.CostEstimate(
            flops=2 * ROWS * 4096 * 2048, bytes_accessed=17 * 2**20, transcendentals=0),
    )(tokens, w_in, short_kernel, residue.T, rate.T, w_out)


def solution(mesh):
    in_specs = (
        P("ctx", "chan"),
        P(None, None, "chan"),
        P(None, None, "chan"),
        P("chan", None),
        P("chan", None),
        P(None, "chan"),
    )
    return jax.shard_map(
        per_device, mesh=mesh, in_specs=in_specs, out_specs=P("ctx", "chan"), check_vma=False)
```

time: 451 us -> 44 us (0.10)
  waiting for transfers between devices: 159 us -> 0 us
  matrix products: 131 us -> 0 us
  local copies, waits for them, and re-layouts: 87.4 us -> 1.67 us
  Pallas kernels: 0 us -> 41.8 us
  starting transfers between devices: 33.3 us -> 0 us
  other arithmetic: 22.7 us -> 0 us
  between operations: 13.6 us -> 0.01 us
    dot_general x20 -> x0, matrix products: 131 us -> none  [the longest x16 92.4 us: sub_states(): jnp.einsum('ckj,cjr->ckr', pieces, tail_power, precision=exact)]
    ppermute x16 -> x0, waiting for transfers between devices: 117 us -> none  [shifted(): return lax.ppermute(value, axis, pairs)]
    pallas_call x0 -> x1, Pallas kernels: none -> 41.8 us  [per_device(): pl.pallas_call(kernel, out_shape=jax.ShapeDtypeStruct((ROWS, WIDE), BF16)...]
    all_gather x2 -> x0, waiting for transfers between devices: 41.5 us -> none  [the longest x1 40.6 us: per_device(): lax.all_gather(modulated, 'chan', axis=1, tiled=True)]
    ppermute x16 -> x0, starting transfers between devices: 33.2 us -> none  [shifted(): return lax.ppermute(value, axis, pairs)]
    gather x2 -> x0, local copies, waits for them, and re-layouts: 33 us -> none  [per_device(): impulse_rows[:, jnp.clip(lagged, 0, sub - 1)]]
    unnamed x21 -> x1, local copies, waits for them, and re-layouts: 18 us -> 1.67 us
    while x16 -> x0, local copies, waits for them, and re-layouts: 10.7 us -> none
  transfers between devices with their start and end apart: 18 -> 0, of which waited for: 17 -> 0; matrix products, arithmetic and copies ran while one was open for 16% -> 0% of each run, Pallas kernels for 0% -> 0%
where the time goes in v2:
time: 44 us; the launch traced here: 43.4 us
  Pallas kernels  41.8 us (95%)
  local copies, waits for them, and re-layouts  1.67 us (4%)
    pallas_call x1, Pallas kernels, per_device(): pl.pallas_call(kernel, out_shape=jax.ShapeDtypeStruct((ROWS, WIDE), BF16)...  41.8 us
    unnamed x1, local copies, waits for them, and re-layouts  1.67 us

profile of v2, /device:TPU:25, one launch (start us, length us, event | category | flops | bytes accessed | tf_op | source)
XLA Modules:
  0.0 43.4 jit_solution(14817777684012218014)
XLA Ops:
  0.0 41.8 %shard_map.64 = bf16[256,512]{1,0:T(8,128)(2,1)} custom-call(bf16[256,512]{1,0:T(8,128)(2,1)} %tok.1, bf16[3,8,512,512]{3,2,1,0:T(8,128)(2,1)} %bitcast.6, f32[3,3,512]{2,1,0:T(4,128)} %taps_hbm.1, f32[16,512]{1,0:T(8,128)} %bitcast.8, f32[16,512]{1,0:T(8,128)} %bitcast.9, bf16[8,512,512]{2,1,0:T(8,128)(2,1)} %bitcast.7), custom_call_target="tpu_custom_call" | custom-call | flops 4294967296 | bytes 17825792 | tf_op jit(solution)/shard_map/pallas_call | solution.py:474
  41.8 1.7 %copy.8 = bf16[256,512]{1,0:T(8,128)(2,1)} copy(bf16[256,512]{1,0:T(8,128)(2,1)} %shard_map.64) | data formatting | bytes 524288

commit v3 on v2

--- a/solution.py
+++ b/solution.py
@@ -8,7 +8,7 @@
 MESH = pl.DeviceIdType.MESH
 F32 = jnp.float32
 BF16 = jnp.bfloat16
-STATE = jnp.float32
+STATE = jnp.bfloat16
 CTX = 16
 ROWS = 256
 WIDE = 512
@@ -86,12 +86,15 @@
             for h in range(2):
                 side[c, h].wait_recv()
 
-    def finish(self):
-        for group in (self.right, self.left, self.own, self.side_l, self.side_r, self.side_f):
-            for c in group.values():
+    def finish(self, late=None):
+        early = [self.right, self.left, self.own, self.side_l, self.side_r]
+        if late is not True:
+            for group in early:
+                for c in group.values():
+                    c.wait_send()
+        if late is not False:
+            for c in list(self.side_f.values()) + self.on_right + self.on_left:
                 c.wait_send()
-        for c in self.on_right + self.on_left:
-            c.wait_send()
 
 
 def total_of(terms):
@@ -181,6 +184,21 @@
         load_w[n].start()
     for n in range(BLOCKS):
         load_o[n].start()
+    @pl.when((ctx < CTX - 1) & (core == 1) & even)
+    def _():
+        pl.semaphore_wait(barrier, 1)
+        for where in (chip(0, 0), chip(1, 0), chip(1, 1)):
+            greet(next_in, where)
+
+    @pl.when((ctx < CTX - 1) & jnp.logical_not((core == 1) & even))
+    def _():
+        pl.semaphore_wait(next_in, 1)
+
+    @pl.when(ctx < CTX - 1)
+    def _():
+        for c in halos:
+            c.start()
+
     for c in load_s:
         c.wait()
 
@@ -193,16 +211,18 @@
         ramp[r] = jnp.exp(-rate[r:r + 1] * (sublane + 1.0)) * weight[r:r + 1]
         run_decay[r] = jnp.exp(-rate[r:r + 1] * (float(SUB) * (float(RUNS - 1) - sublane)))
 
-    def project(n, part=None, fresh=False, slots=(0, 1, 2), last=False):
+    ALL, BODY, TOP = slice(0, HEAD + ROWS), slice(HEAD, HEAD + ROWS), slice(0, HEAD)
+
+    def project(n, part=None, rows=ALL, fresh=False, slots=(0, 1, 2), last=False):
         b = order[n]
         cols = slice(0, WIDE) if part is None else slice(part * HALF, (part + 1) * HALF)
         for s in slots:
-            value = jnp.dot(gat[b, :, cols], win[s, b, cols], preferred_element_type=F32)
+            value = jnp.dot(gat[b, rows, cols], win[s, b, cols], preferred_element_type=F32)
             if not fresh:
-                value = acc[s] + value
+                value = acc[s, rows] + value
             if last:
                 value = value.astype(BF16).astype(F32)
-            acc[s] = value
+            acc[s, rows] = value
 
     def take_halo():
         @pl.when(ctx > 0)
@@ -220,54 +240,42 @@
 
     def project_own():
         load_w[0].wait()
-        project(0, fresh=True)
+        project(0, rows=BODY, fresh=True)
 
     def project_other():
         load_w[1].wait()
         for c in range(2):
             g1.wait_side([g1.own], c)
-        project(1)
+        project(1, rows=BODY)
 
     def project_near():
         load_w[2].wait()
-        project(2)
+        project(2, rows=BODY)
         load_w[3].wait()
-        project(3)
+        project(3, rows=BODY)
 
     def project_near_other():
+        hear_later()
+        take_halo()
         for c in range(2):
             g1.wait_side([g1.side_l, g1.side_r], c)
+        project(0, rows=TOP, fresh=True)
+        project(1, rows=TOP)
         load_w[4].wait()
         project(4)
 
     def project_far():
         load_w[5].wait()
         project(5)
+        project(2, rows=TOP)
+        project(3, rows=TOP)
         load_w[6].wait()
-        project(6, 0)
+        project(6)
         load_w[7].wait()
         g1.wait_side([g1.side_f], 0)
         project(7, 0)
-        project(6, 1)
         g1.wait_side([g1.side_f], 1)
         project(7, 1, slots=(1, 2), last=True)
-
-    def hear_next():
-        @pl.when((ctx < CTX - 1) & (core == 1) & even)
-        def _():
-            pl.semaphore_wait(barrier, 1)
-            for where in (chip(0, 0), chip(1, 0), chip(1, 1)):
-                greet(next_in, where)
-
-    def send_halo():
-        @pl.when((ctx < CTX - 1) & jnp.logical_not((core == 1) & even))
-        def _():
-            pl.semaphore_wait(next_in, 1)
-
-        @pl.when(ctx < CTX - 1)
-        def _():
-            for c in halos:
-                c.start()
 
     def hear_later():
         @pl.when((ctx < CTX - 1) & (core == 1) & jnp.logical_not(even))
@@ -279,17 +287,7 @@
     def idle():
         pass
 
-    def project_first():
-        take_halo()
-        project_own()
-        project_other()
-
-    def project_middle():
-        hear_later()
-        project_near()
-        project_near_other()
-
-    g1.relay((hear_next, send_halo, idle, idle, project_first, project_middle, project_far))
+    g1.relay((idle, project_own, project_other, idle, project_near, project_near_other, project_far))
 
     def filtered(s, q, lanes):
         value = None
@@ -377,9 +375,6 @@
 
             lax.fori_loop(0, SUB, step, tuple(before), unroll=2)
 
-    own_part(0)
-    own_part(1)
-
     def merge(half):
         def add(j, value):
             remote(state_out.at[half], state_in.at[half, j], state_send.at[half, 0], state_recv.at[half, j],
@@ -408,6 +403,7 @@
 
     g2 = Gather(lambda c, h: mod.at[me, pl.ds(h * TALL, TALL), pl.ds(c * HALF, HALF)], mod, 0, *ring, send2, recv2)
     for half in range(2):
+        own_part(half)
         merge(half)
         modulate(half)
         g2.begin(half)
@@ -417,6 +413,21 @@
         cols = slice(0, WIDE) if part is None else slice(part * HALF, (part + 1) * HALF)
         value = jnp.dot(mod[b, :, cols], wout[b, cols], preferred_element_type=F32)
         total[...] = value if fresh else total[...] + value
+
+    def settle():
+        g1.finish()
+
+        @pl.when(ctx < CTX - 1)
+        def _():
+            for c in halos:
+                c.wait_send()
+
+        for half in range(2):
+            for ahead in range(1, CTX):
+                @pl.when(ctx + ahead < CTX)
+                def _():
+                    remote(state_out.at[half], state_in.at[half, ctx], state_send.at[half, ahead],
+                           state_recv.at[half, ctx], (lax.rem(ctx + ahead, CTX), me)).wait_send()
 
     def mix_own():
         for c in load_o:
@@ -438,6 +449,7 @@
         mix(4)
         mix(5)
         mix(6, 0)
+        g2.finish(late=False)
 
     def mix_far():
         g2.wait_side([g2.side_f], 0)
@@ -448,22 +460,9 @@
         out[...] = (total[...] + jnp.dot(
             mod[b, :, HALF:], wout[b, HALF:], preferred_element_type=F32)).astype(BF16)
 
-    g2.relay((idle, mix_own, mix_other, idle, mix_near, mix_near_other, mix_far))
-
-    g1.finish()
-    g2.finish()
-
-    @pl.when(ctx < CTX - 1)
-    def _():
-        for c in halos:
-            c.wait_send()
-
-    for half in range(2):
-        for ahead in range(1, CTX):
-            @pl.when(ctx + ahead < CTX)
-            def _():
-                remote(state_out.at[half], state_in.at[half, ctx], state_send.at[half, ahead],
-                       state_recv.at[half, ctx], (lax.rem(ctx + ahead, CTX), me)).wait_send()
+    g2.relay((settle, mix_own, mix_other, idle, mix_near, mix_near_other, mix_far))
+
+    g2.finish(late=True)
 
 
 def per_device(tokens, w_in, short_kernel, residue, rate, w_out):
@@ -473,7 +472,7 @@
     vmem = pltpu.VMEM
     return pl.pallas_call(
         kernel,
-        out_shape=jax.ShapeDtypeStruct((ROWS, WIDE), BF16),
+        out_shape=pltpu.VMEM((ROWS, WIDE), BF16),
         in_specs=[pl.BlockSpec(memory_space=pltpu.HBM)] * 6,
         out_specs=pl.BlockSpec(memory_space=pltpu.VMEM),
         scratch_shapes=[

time: 44 us -> 39.2 us (0.89); the launches traced: 43.4 us -> 39.1 us
  Pallas kernels: 41.8 us -> 38.4 us
  local copies, waits for them, and re-layouts: 1.67 us -> 0.71 us
    pallas_call x1, Pallas kernels: 41.8 us -> 38.4 us  [per_device(): pl.pallas_call(kernel, out_shape=pltpu.VMEM((ROWS, WIDE), BF16), in_specs...]
    unnamed x1, local copies, waits for them, and re-layouts: 1.67 us -> 0.71 us
where the time goes in v3:
time: 39.2 us; the launch traced here: 39.1 us
  Pallas kernels  38.4 us (98%)
  local copies, waits for them, and re-layouts  0.71 us (2%)
    pallas_call x1, Pallas kernels, per_device(): pl.pallas_call(kernel, out_shape=pltpu.VMEM((ROWS, WIDE), BF16), in_specs...  38.4 us

profile of v3, /device:TPU:25, one launch (start us, length us, event | category | flops | bytes accessed | tf_op | source)
XLA Modules:
  0.0 39.1 jit_solution(10967369591702010131)
XLA Ops:
  0.0 38.4 %shard_map.64 = bf16[256,512]{1,0:T(8,128)(2,1)S(1)} custom-call(bf16[256,512]{1,0:T(8,128)(2,1)} %tok.1, bf16[3,8,512,512]{3,2,1,0:T(8,128)(2,1)} %bitcast.6, f32[3,3,512]{2,1,0:T(4,128)} %taps_hbm.1, f32[16,512]{1,0:T(8,128)} %bitcast.8, f32[16,512]{1,0:T(8,128)} %bitcast.9, bf16[8,512,512]{2,1,0:T(8,128)(2,1)} %bitcast.7), custom_call_target="tpu_custom_call" | custom-call | flops 4294967296 | bytes 17825792 | tf_op jit(solution)/shard_map/pallas_call | solution.py:473
  38.4 0.7 %copy.8 = bf16[256,512]{1,0:T(8,128)(2,1)} copy(bf16[256,512]{1,0:T(8,128)(2,1)S(1)} %shard_map.64) | data formatting | bytes 524288

commit v4 on v3

--- a/solution.py
+++ b/solution.py
@@ -22,6 +22,7 @@
 HALF = WIDE // 2
 TALL = ROWS // 2
 HEAD = 16
+SPLIT = (0, 2, TILES)
 
 
 def remote(src, dst, send, recv, where):
@@ -30,16 +31,13 @@
 
 
 class Gather:
-    def __init__(self, source, store, top, block, left, right, far, dev, send, recv):
+    def __init__(self, source, here, block, left, right, far, dev, send, recv):
         count = [0]
 
         def copy(src, dst, where):
             s = count[0]
             count[0] += 1
             return remote(src, dst, send.at[s], recv.at[s], where)
-
-        def here(owner, c, h):
-            return store.at[owner, pl.ds(top + h * TALL, TALL), pl.ds(c * HALF, HALF)]
 
         quarters = [(c, h) for c in range(2) for h in range(2)]
         to_right, to_left, to_other = dev(1), dev(3), dev(0, True)
@@ -58,6 +56,13 @@
             self.left[c, 1 - h].start()
         for h in range(2):
             self.own[c, h].start()
+
+    def begin_rows(self, c, h):
+        self.right[c, h].start()
+        if h == 1:
+            self.left[c, 1].start()
+            self.left[c, 0].start()
+        self.own[c, h].start()
 
     def relay(self, work):
         work[0]()
@@ -105,9 +110,10 @@
 
 def kernel(tok, w_in, taps_hbm, residue_hbm, rate_hbm, w_out, out,
            taps, residue, rate, win, wout, gat, mod, acc, total, gated, conv, gate0,
-           decay, weight, run_state, run_decay, ramp, halo_out, halo_in, state_out, state_in, entry,
+           decay, weight, run_state, run_decay, ramp, halo_out, halo_in, state_out0, state_out1, state_in0, state_in1, entry,
            w_sems, o_sems, own_sem, small_sems, send1, recv1, send2, recv2, halo_send, halo_recv,
-           state_send, state_recv, ready, next_in, later_in):
+           state_send, state_recv, ready, ring_in, next_in, later_in):
+    state_out, state_in = (state_out0, state_out1), (state_in0, state_in1)
     me = lax.axis_index("chan")
     ctx = lax.axis_index("ctx")
     x, core = me // 2, me % 2
@@ -122,7 +128,8 @@
 
     load_w = [pltpu.make_async_copy(w_in.at[:, b], win.at[:, b], w_sems.at[n]) for n, b in enumerate(order)]
     load_o = [pltpu.make_async_copy(w_out.at[b], wout.at[b], o_sems.at[n]) for n, b in enumerate(order)]
-    load_t = pltpu.make_async_copy(tok, gat.at[me, pl.ds(HEAD, ROWS)], own_sem)
+    load_t = [pltpu.make_async_copy(tok.at[:, pl.ds(c * HALF, HALF)], gat.at[me, c, pl.ds(HEAD, ROWS)], own_sem.at[c])
+              for c in range(2)]
     load_s = [pltpu.make_async_copy(src, dst, small_sems.at[n]) for n, (src, dst) in enumerate(
         ((rate_hbm, rate), (residue_hbm, residue), (taps_hbm, taps)))]
 
@@ -133,71 +140,81 @@
 
     def chip(step, of_core):
         return (ctx, lax.rem(x + step, 4) * 2 + of_core)
-
-    load_t.start()
-    for c in load_s:
-        c.start()
 
     @pl.when(core == 0)
     def _():
         greet(barrier, chip(1, 0))
         greet(barrier, chip(3, 0))
-        pl.semaphore_wait(barrier, 5)
-        for step in (0, 1, 3):
-            greet(ready, chip(step, 1))
 
     @pl.when(core == 1)
     def _():
         for step in (0, 1, 3):
             greet(barrier, chip(step, 0))
-        pl.semaphore_wait(ready, 3)
+
+    for c in load_t + load_s + load_w + load_o:
+        c.start()
+
+    @pl.when(core == 0)
+    def _():
+        pl.semaphore_wait(barrier, 5)
+        greet(ready, chip(0, 1))
+        greet(ring_in, chip(1, 1))
+        greet(ring_in, chip(3, 1))
+
+    @pl.when(core == 1)
+    def _():
+        pl.semaphore_wait(ready, 1)
 
     ring = (me, at(3), at(1), at(2), dev)
-    g1 = Gather(lambda c, h: tok.at[pl.ds(h * TALL, TALL), pl.ds(c * HALF, HALF)], gat, HEAD, *ring, send1, recv1)
+    g1 = Gather(lambda c, h: tok.at[pl.ds(h * TALL, TALL), pl.ds(c * HALF, HALF)],
+                lambda b, c, h: gat.at[b, c, pl.ds(HEAD + h * TALL, TALL)], *ring, send1, recv1)
     g1.begin(0)
     g1.begin(1)
 
     even = lax.rem(x, 2) == 0
+
+    @pl.when(core == 1)
+    def _():
+        pl.semaphore_wait(ring_in, 2)
 
     @pl.when((core == 1) & even & (ctx > 0))
     def _():
         greet(barrier, (ctx - 1, me))
 
-    for back in range(1, CTX):
-        @pl.when((core == 1) & jnp.logical_not(even) & (ctx >= back))
-        def _():
-            greet(barrier, (ctx - back, me))
-
-    load_w[0].start()
-    load_w[1].start()
-    load_t.wait()
+    for c in load_t:
+        c.wait()
     row16 = lax.broadcasted_iota(jnp.int32, (HEAD, LANES), 0)
     packed = jnp.zeros((HEAD, LANES), F32)
     for t in range(TILES):
-        last = gat[me, ROWS:ROWS + HEAD, t * LANES:(t + 1) * LANES].astype(F32)
+        last = gat[me, t // 2, ROWS:ROWS + HEAD, t % 2 * LANES:(t % 2 + 1) * LANES].astype(F32)
         packed = jnp.where(row16 // 2 == t, pltpu.roll(last, 2 * t + 2, 0), packed)
     halo_out[...] = packed.astype(BF16)
     halos = [remote(halo_out, halo_in.at[me], halo_send.at[o], halo_recv.at[me],
                     (lax.rem(ctx + 1, CTX), lax.rem(me + o, BLOCKS))) for o in range(BLOCKS)]
 
-    for n in range(2, BLOCKS):
-        load_w[n].start()
-    for n in range(BLOCKS):
-        load_o[n].start()
-    @pl.when((ctx < CTX - 1) & (core == 1) & even)
-    def _():
-        pl.semaphore_wait(barrier, 1)
-        for where in (chip(0, 0), chip(1, 0), chip(1, 1)):
-            greet(next_in, where)
-
-    @pl.when((ctx < CTX - 1) & jnp.logical_not((core == 1) & even))
-    def _():
-        pl.semaphore_wait(next_in, 1)
-
-    @pl.when(ctx < CTX - 1)
-    def _():
-        for c in halos:
-            c.start()
+    def send_halo(now):
+        @pl.when(now & (core == 1) & even)
+        def _():
+            pl.semaphore_wait(barrier, 1)
+            for where in (chip(0, 0), chip(1, 0), chip(1, 1)):
+                greet(next_in, where)
+
+        @pl.when(now & jnp.logical_not((core == 1) & even))
+        def _():
+            pl.semaphore_wait(next_in, 1)
+
+        @pl.when(now)
+        def _():
+            for c in halos:
+                c.start()
+
+    waits_long = lax.rem(ctx, 4) != 3
+    send_halo((ctx < CTX - 1) & jnp.logical_not(waits_long))
+
+    for back in range(1, CTX):
+        @pl.when((core == 1) & jnp.logical_not(even) & (ctx >= back))
+        def _():
+            greet(barrier, (ctx - back, me))
 
     for c in load_s:
         c.wait()
@@ -211,13 +228,18 @@
         ramp[r] = jnp.exp(-rate[r:r + 1] * (sublane + 1.0)) * weight[r:r + 1]
         run_decay[r] = jnp.exp(-rate[r:r + 1] * (float(SUB) * (float(RUNS - 1) - sublane)))
 
+    def halves_of(store, b, part, rows):
+        if part is None:
+            return jnp.concatenate([store[b, 0, rows], store[b, 1, rows]], 1)
+        return store[b, part, rows]
+
     ALL, BODY, TOP = slice(0, HEAD + ROWS), slice(HEAD, HEAD + ROWS), slice(0, HEAD)
 
     def project(n, part=None, rows=ALL, fresh=False, slots=(0, 1, 2), last=False):
         b = order[n]
         cols = slice(0, WIDE) if part is None else slice(part * HALF, (part + 1) * HALF)
         for s in slots:
-            value = jnp.dot(gat[b, rows, cols], win[s, b, cols], preferred_element_type=F32)
+            value = jnp.dot(halves_of(gat, b, part, rows), win[s, b, cols], preferred_element_type=F32)
             if not fresh:
                 value = acc[s, rows] + value
             if last:
@@ -225,20 +247,24 @@
             acc[s, rows] = value
 
     def take_halo():
+        acc[:, TOP] = jnp.zeros((3, HEAD, WIDE), F32)
+
         @pl.when(ctx > 0)
         def _():
             for q in range(BLOCKS):
                 remote(halo_out, halo_in.at[q], halo_send.at[0], halo_recv.at[q], dev(1)).wait_recv()
                 rows = halo_in[q].astype(F32)
                 for t in range(TILES):
-                    gat[q, 0:HEAD, t * LANES:(t + 1) * LANES] = pltpu.roll(rows, HEAD - 2 - 2 * t, 0).astype(BF16)
+                    gat[q, t // 2, 0:HEAD, t % 2 * LANES:(t % 2 + 1) * LANES] = pltpu.roll(
+                        rows, HEAD - 2 - 2 * t, 0).astype(BF16)
 
         @pl.when(ctx == 0)
         def _():
             for q in range(BLOCKS):
-                gat[q, 0:HEAD] = jnp.zeros((HEAD, WIDE), BF16)
+                gat[q, :, 0:HEAD] = jnp.zeros((2, HEAD, HALF), BF16)
 
     def project_own():
+        send_halo((ctx < CTX - 1) & waits_long)
         load_w[0].wait()
         project(0, rows=BODY, fresh=True)
 
@@ -259,16 +285,14 @@
         take_halo()
         for c in range(2):
             g1.wait_side([g1.side_l, g1.side_r], c)
-        project(0, rows=TOP, fresh=True)
-        project(1, rows=TOP)
         load_w[4].wait()
         project(4)
-
-    def project_far():
         load_w[5].wait()
         project(5)
-        project(2, rows=TOP)
-        project(3, rows=TOP)
+
+    def project_far():
+        for n in range(4):
+            project(n, rows=TOP)
         load_w[6].wait()
         project(6)
         load_w[7].wait()
@@ -302,17 +326,20 @@
     def spread(ref, r, lanes):
         return jnp.broadcast_to(ref[r:r + 1, lanes], (8, LANES))
 
+    def columns(half):
+        return slice(SPLIT[half] * LANES, SPLIT[half + 1] * LANES)
+
     def lanes_of(tile):
         return pl.ds(pl.multiple_of(tile * LANES, LANES), LANES)
 
     def block_state(half):
-        for t in range(2 * half, 2 * half + 2):
+        for t in range(SPLIT[half], SPLIT[half + 1]):
             lanes = slice(t * LANES, (t + 1) * LANES)
             for q in range(RUNS):
                 gated[t, SUB * q:SUB * (q + 1)] = (
                     filtered(1, q, lanes) * filtered(2, q, lanes)).astype(BF16).astype(F32)
 
-        @pl.loop(2 * half, 2 * half + 2)
+        @pl.loop(SPLIT[half], SPLIT[half + 1])
         def _(tile):
             lanes = lanes_of(tile)
             d = [spread(decay.at[0], r, lanes) for r in range(MODES)]
@@ -321,11 +348,11 @@
                 g = gated[tile, pl.ds(j, RUNS, stride=SUB)]
                 return tuple(d[r] * states[r] + g for r in range(MODES))
 
-            states = lax.fori_loop(0, SUB, step, tuple(jnp.zeros((8, LANES), F32) for _ in range(MODES)), unroll=8)
-            where = pl.ds(pl.multiple_of((tile - 2 * half) * LANES, LANES), LANES)
+            states = lax.fori_loop(0, SUB, step, tuple(jnp.zeros((8, LANES), F32) for _ in range(MODES)), unroll=32)
+            where = pl.ds(pl.multiple_of((tile - SPLIT[half]) * LANES, LANES), LANES)
             for r in range(MODES):
                 run_state[r, :, lanes] = states[r]
-                state_out[half, r:r + 1, where] = jnp.sum(
+                state_out[half][r:r + 1, where] = jnp.sum(
                     run_decay[r, :, lanes] * states[r], axis=0, keepdims=True).astype(STATE)
 
         if half == 0:
@@ -336,7 +363,7 @@
         for ahead in range(1, CTX):
             @pl.when(ctx + ahead < CTX)
             def _():
-                remote(state_out.at[half], state_in.at[half, ctx], state_send.at[half, ahead], state_recv.at[half, ctx],
+                remote(state_out[half], state_in[half].at[ctx], state_send.at[half, ahead], state_recv.at[half, ctx],
                        (lax.rem(ctx + ahead, CTX), me)).start()
 
     block_state(0)
@@ -344,12 +371,12 @@
     project(7, 1, slots=(0,), last=True)
 
     def own_part(half):
-        for t in range(2 * half, 2 * half + 2):
+        for t in range(SPLIT[half], SPLIT[half + 1]):
             lanes = slice(t * LANES, (t + 1) * LANES)
             for q in range(RUNS):
                 gate0[t, SUB * q:SUB * (q + 1)] = filtered(0, q, lanes)
 
-        @pl.loop(2 * half, 2 * half + 2)
+        @pl.loop(SPLIT[half], SPLIT[half + 1])
         def _(tile):
             lanes = lanes_of(tile)
             before = []
@@ -373,21 +400,25 @@
                 conv[tile, pl.ds(j, RUNS, stride=SUB)] = total_of(sums)
                 return tuple(after)
 
-            lax.fori_loop(0, SUB, step, tuple(before), unroll=2)
+            lax.fori_loop(0, SUB, step, tuple(before), unroll=8)
 
     def merge(half):
         def add(j, value):
-            remote(state_out.at[half], state_in.at[half, j], state_send.at[half, 0], state_recv.at[half, j],
+            remote(state_out[half], state_in[half].at[j], state_send.at[half, 0], state_recv.at[half, j],
                    dev(1)).wait_recv()
-            return decay[5, :, half * HALF:(half + 1) * HALF] * value + state_in[half, j].astype(F32)
-
-        entry[:, half * HALF:(half + 1) * HALF] = lax.fori_loop(0, ctx, add, jnp.zeros((MODES, HALF), F32))
-
-    def modulate(half):
-        @pl.loop(2 * half, 2 * half + 2)
+            return decay[5, :, columns(half)] * value + state_in[half][j].astype(F32)
+
+        cols = columns(half)
+        entry[:, cols] = lax.fori_loop(0, ctx, add, jnp.zeros((MODES, cols.stop - cols.start), F32))
+
+    def modulate(half, high):
+        @pl.loop(SPLIT[half], SPLIT[half + 1])
         def _(tile):
             lanes = lanes_of(tile)
-            z = tuple(ramp[r, :, lanes] * entry[r:r + 1, lanes] for r in range(MODES))
+            if high == 0:
+                z = tuple(ramp[r, :, lanes] * entry[r:r + 1, lanes] for r in range(MODES))
+            else:
+                z = tuple(run_state[r, :, lanes] for r in range(MODES))
             d8 = [spread(decay.at[1], r, lanes) for r in range(MODES)]
 
             def step(q, z):
@@ -399,18 +430,27 @@
                 mod[me, pl.ds(pl.multiple_of(q * 16, 16), 16), lanes] = jnp.concatenate(halves, 0).astype(BF16)
                 return z
 
-            lax.fori_loop(0, ROWS // 16, step, z, unroll=2)
-
-    g2 = Gather(lambda c, h: mod.at[me, pl.ds(h * TALL, TALL), pl.ds(c * HALF, HALF)], mod, 0, *ring, send2, recv2)
+            z = lax.fori_loop(high * TALL // 16, (high + 1) * TALL // 16, step, z, unroll=2)
+            if high == 0:
+                for r in range(MODES):
+                    run_state[r, :, lanes] = z[r]
+
+    def place(b, c, h):
+        cols = columns(c)
+        return mod.at[b, pl.ds(h * TALL, TALL), pl.ds(cols.start, cols.stop - cols.start)]
+
+    g2 = Gather(lambda c, h: place(me, c, h), place, *ring, send2, recv2)
     for half in range(2):
         own_part(half)
         merge(half)
-        modulate(half)
-        g2.begin(half)
+        modulate(half, 0)
+        g2.begin_rows(half, 0)
+        modulate(half, 1)
+        g2.begin_rows(half, 1)
 
     def mix(n, part=None, fresh=False):
         b = order[n]
-        cols = slice(0, WIDE) if part is None else slice(part * HALF, (part + 1) * HALF)
+        cols = slice(0, WIDE) if part is None else columns(part)
         value = jnp.dot(mod[b, :, cols], wout[b, cols], preferred_element_type=F32)
         total[...] = value if fresh else total[...] + value
 
@@ -426,7 +466,7 @@
             for ahead in range(1, CTX):
                 @pl.when(ctx + ahead < CTX)
                 def _():
-                    remote(state_out.at[half], state_in.at[half, ctx], state_send.at[half, ahead],
+                    remote(state_out[half], state_in[half].at[ctx], state_send.at[half, ahead],
                            state_recv.at[half, ctx], (lax.rem(ctx + ahead, CTX), me)).wait_send()
 
     def mix_own():
@@ -449,18 +489,18 @@
         mix(4)
         mix(5)
         mix(6, 0)
-        g2.finish(late=False)
 
     def mix_far():
         g2.wait_side([g2.side_f], 0)
         mix(7, 0)
         mix(6, 1)
+        g2.finish(late=False)
         g2.wait_side([g2.side_f], 1)
         b = order[7]
         out[...] = (total[...] + jnp.dot(
-            mod[b, :, HALF:], wout[b, HALF:], preferred_element_type=F32)).astype(BF16)
-
-    g2.relay((settle, mix_own, mix_other, idle, mix_near, mix_near_other, mix_far))
+            mod[b, :, columns(1)], wout[b, columns(1)], preferred_element_type=F32)).astype(BF16)
+
+    g2.relay((idle, mix_own, mix_other, settle, mix_near, mix_near_other, mix_far))
 
     g2.finish(late=True)
 
@@ -481,7 +521,7 @@
             vmem((MODES, WIDE), F32),
             vmem((3, BLOCKS, WIDE, WIDE), BF16),
             vmem((BLOCKS, WIDE, WIDE), BF16),
-            vmem((BLOCKS, HEAD + ROWS, WIDE), BF16),
+            vmem((BLOCKS, 2, HEAD + ROWS, HALF), BF16),
             vmem((BLOCKS, ROWS, WIDE), BF16),
             vmem((3, HEAD + ROWS, WIDE), F32),
             vmem((ROWS, WIDE), F32),
@@ -495,14 +535,15 @@
             vmem((MODES, 8, WIDE), F32),
             vmem((HEAD, LANES), BF16),
             vmem((BLOCKS, HEAD, LANES), BF16),
-            vmem((2, MODES, HALF), STATE),
-            vmem((2, CTX, MODES, HALF), STATE),
+            *[vmem((MODES, (SPLIT[h + 1] - SPLIT[h]) * LANES), STATE) for h in range(2)],
+            *[vmem((CTX, MODES, (SPLIT[h + 1] - SPLIT[h]) * LANES), STATE) for h in range(2)],
             vmem((MODES, WIDE), F32),
-            dma((BLOCKS,)), dma((BLOCKS,)), dma, dma((3,)),
+            dma((BLOCKS,)), dma((BLOCKS,)), dma((2,)), dma((3,)),
             dma((32,)), dma((32,)), dma((32,)), dma((32,)),
             dma((BLOCKS,)), dma((BLOCKS,)),
             dma((2, CTX)), dma((2, CTX)),
             pltpu.SemaphoreType.REGULAR, pltpu.SemaphoreType.REGULAR, pltpu.SemaphoreType.REGULAR,
+            pltpu.SemaphoreType.REGULAR,
         ],
         compiler_params=pltpu.CompilerParams(
             collective_id=0, has_side_effects=True, vmem_limit_bytes=60 * 2**20),

time: 39.2 us -> 38.9 us (level)
  Pallas kernels: 38.4 us -> 38 us
    pallas_call x1, Pallas kernels: 38.4 us -> 38 us  [per_device(): pl.pallas_call(kernel, out_shape=pltpu.VMEM((ROWS, WIDE), BF16), in_specs...]
where the time goes in v4:
time: 38.9 us; the launch traced here: 38.7 us
  Pallas kernels  38 us (98%)
  local copies, waits for them, and re-layouts  0.71 us (2%)
    pallas_call x1, Pallas kernels, per_device(): pl.pallas_call(kernel, out_shape=pltpu.VMEM((ROWS, WIDE), BF16), in_specs...  38 us

profile of v4, /device:TPU:25, one launch (start us, length us, event | category | flops | bytes accessed | tf_op | source)
XLA Modules:
  0.0 38.7 jit_solution(790263920534342022)
XLA Ops:
  0.0 38.0 %shard_map.64 = bf16[256,512]{1,0:T(8,128)(2,1)S(1)} custom-call(bf16[256,512]{1,0:T(8,128)(2,1)} %tok.1, bf16[3,8,512,512]{3,2,1,0:T(8,128)(2,1)} %bitcast.6, f32[3,3,512]{2,1,0:T(4,128)} %taps_hbm.1, f32[16,512]{1,0:T(8,128)} %bitcast.8, f32[16,512]{1,0:T(8,128)} %bitcast.9, bf16[8,512,512]{2,1,0:T(8,128)(2,1)} %bitcast.7), custom_call_target="tpu_custom_call" | custom-call | flops 4294967296 | bytes 17825792 | tf_op jit(solution)/shard_map/pallas_call | solution.py:513
  38.0 0.7 %copy.8 = bf16[256,512]{1,0:T(8,128)(2,1)} copy(bf16[256,512]{1,0:T(8,128)(2,1)S(1)} %shard_map.64) | data formatting | bytes 524288

commit v5 on v4

--- a/solution.py
+++ b/solution.py
@@ -151,7 +151,7 @@
         for step in (0, 1, 3):
             greet(barrier, chip(step, 0))
 
-    for c in load_t + load_s + load_w + load_o:
+    for c in load_t + load_s:
         c.start()
 
     @pl.when(core == 0)
@@ -166,10 +166,16 @@
         pl.semaphore_wait(ready, 1)
 
     ring = (me, at(3), at(1), at(2), dev)
-    g1 = Gather(lambda c, h: tok.at[pl.ds(h * TALL, TALL), pl.ds(c * HALF, HALF)],
-                lambda b, c, h: gat.at[b, c, pl.ds(HEAD + h * TALL, TALL)], *ring, send1, recv1)
+    def place_token(b, c, h):
+        return gat.at[b, c, pl.ds(HEAD + h * TALL, TALL)]
+
+    for c in load_t:
+        c.wait()
+    g1 = Gather(lambda c, h: place_token(me, c, h), place_token, *ring, send1, recv1)
     g1.begin(0)
     g1.begin(1)
+    for c in load_w:
+        c.start()
 
     even = lax.rem(x, 2) == 0
 
@@ -181,8 +187,6 @@
     def _():
         greet(barrier, (ctx - 1, me))
 
-    for c in load_t:
-        c.wait()
     row16 = lax.broadcasted_iota(jnp.int32, (HEAD, LANES), 0)
     packed = jnp.zeros((HEAD, LANES), F32)
     for t in range(TILES):
@@ -366,6 +370,8 @@
                 remote(state_out[half], state_in[half].at[ctx], state_send.at[half, ahead], state_recv.at[half, ctx],
                        (lax.rem(ctx + ahead, CTX), me)).start()
 
+    for c in load_o:
+        c.start()
     block_state(0)
     block_state(1)
     project(7, 1, slots=(0,), last=True)

time: 38.9 us -> 38.7 us (level)
  no operation moved by 1% of the time
where the time goes in v5:
time: 38.7 us; the launch traced here: 38.5 us
  Pallas kernels  37.8 us (98%)
  local copies, waits for them, and re-layouts  0.71 us (2%)
    pallas_call x1, Pallas kernels, per_device(): pl.pallas_call(kernel, out_shape=pltpu.VMEM((ROWS, WIDE), BF16), in_specs...  37.8 us

profile of v5, /device:TPU:25, one launch (start us, length us, event | category | flops | bytes accessed | tf_op | source)
XLA Modules:
  0.0 38.5 jit_solution(13063292638034402221)
XLA Ops:
  0.0 37.8 %shard_map.64 = bf16[256,512]{1,0:T(8,128)(2,1)S(1)} custom-call(bf16[256,512]{1,0:T(8,128)(2,1)} %tok.1, bf16[3,8,512,512]{3,2,1,0:T(8,128)(2,1)} %bitcast.6, f32[3,3,512]{2,1,0:T(4,128)} %taps_hbm.1, f32[16,512]{1,0:T(8,128)} %bitcast.8, f32[16,512]{1,0:T(8,128)} %bitcast.9, bf16[8,512,512]{2,1,0:T(8,128)(2,1)} %bitcast.7), custom_call_target="tpu_custom_call" | custom-call | flops 4294967296 | bytes 17825792 | tf_op jit(solution)/shard_map/pallas_call | solution.py:519
  37.8 0.7 %copy.8 = bf16[256,512]{1,0:T(8,128)(2,1)} copy(bf16[256,512]{1,0:T(8,128)(2,1)S(1)} %shard_map.64) | data formatting | bytes 524288

commit v6 on v5

--- a/solution.py
+++ b/solution.py
@@ -446,8 +446,9 @@
         return mod.at[b, pl.ds(h * TALL, TALL), pl.ds(cols.start, cols.stop - cols.start)]
 
     g2 = Gather(lambda c, h: place(me, c, h), place, *ring, send2, recv2)
+    own_part(0)
+    own_part(1)
     for half in range(2):
-        own_part(half)
         merge(half)
         modulate(half, 0)
         g2.begin_rows(half, 0)

time: 38.7 us -> 38.7 us (level)
  no operation moved by 1% of the time
where the time goes in v6:
time: 38.7 us; the launch traced here: 38.3 us
  Pallas kernels  37.6 us (97%)
  local copies, waits for them, and re-layouts  0.71 us (2%)
    pallas_call x1, Pallas kernels, per_device(): pl.pallas_call(kernel, out_shape=pltpu.VMEM((ROWS, WIDE), BF16), in_specs...  37.6 us

profile of v6, /device:TPU:25, one launch (start us, length us, event | category | flops | bytes accessed | tf_op | source)
XLA Modules:
  0.0 38.3 jit_solution(12613814447398919917)
XLA Ops:
  0.0 37.6 %shard_map.64 = bf16[256,512]{1,0:T(8,128)(2,1)S(1)} custom-call(bf16[256,512]{1,0:T(8,128)(2,1)} %tok.1, bf16[3,8,512,512]{3,2,1,0:T(8,128)(2,1)} %bitcast.6, f32[3,3,512]{2,1,0:T(4,128)} %taps_hbm.1, f32[16,512]{1,0:T(8,128)} %bitcast.8, f32[16,512]{1,0:T(8,128)} %bitcast.9, bf16[8,512,512]{2,1,0:T(8,128)(2,1)} %bitcast.7), custom_call_target="tpu_custom_call" | custom-call | flops 4294967296 | bytes 17825792 | tf_op jit(solution)/shard_map/pallas_call | solution.py:520
  37.6 0.7 %copy.8 = bf16[256,512]{1,0:T(8,128)(2,1)} copy(bf16[256,512]{1,0:T(8,128)(2,1)S(1)} %shard_map.64) | data formatting | bytes 524288
